TPU v7x, 256 devices: a whole 4x4x8 slice. The times are simulated.
256 devices in a mesh: row: 8 (over z_lo, core), col: 32 (over z_hi, y, x).
Axes of the slice: x: 4, y: 4, z: 8 (z_hi: 2, z_lo: 4; z = z_hi * 4 + z_lo), core: 2. Of those that a mesh axis runs over, the one named last changes fastest.
Arguments:
- observations: float32 [8192, 16, 4096], P('row', None, 'col'), may hold values from -6 to 6
- prior_rows: float32 [256, 16, 4096], P(None, 'row', 'col'), may hold values from -8 to 96, as said below
Outputs:
- updated_rows: float32 [256, 16, 4096], P(None, 'row', 'col')
Inputs may be any that keep to these rules, and one draw needn't show every extreme that they name: `prior_rows`: entry (i, c, q) is zero where its global column is below i, lies in [32, 96] where the global column equals i, and elsewhere lies in [-8, 8].
All inputs are finite; a program needn't handle non-finite values.
Results may differ from a plain program's by a relative error of at most 0.0001.
Values sent between devices are 32-bit elements; how exact they have to be, the bound alone decides.
No kernel may reach another device: no remote copies, remote signals or barrier semaphores. Data moves between devices by JAX's collectives and lax.ppermute only.
A program may use at most 128 MiB of HBM per device.

v0:
```python
import jax
import jax.numpy as jnp
from jax import lax
from jax.sharding import PartitionSpec as P

highest_precision = lax.Precision.HIGHEST


def spread(x, axis, root):
    mine = lax.axis_index(axis) == root
    return lax.psum(jnp.where(mine, x, jnp.zeros_like(x)), axis)


def local(observations, prior_rows):
    tile_size = observations.shape[2]
    cycles = observations.shape[1]
    own_cycles = prior_rows.shape[1]
    panels = prior_rows.shape[0] // tile_size
    n_cols = lax.axis_size("col")
    row_pos = lax.axis_index("row")
    col_pos = lax.axis_index("col")
    first_cycle = row_pos * own_cycles
    holder = row_pos == 0
    measurement_rows = observations
    prior_factor_rows = prior_rows
    block_ids = (
        first_cycle + lax.broadcasted_iota(jnp.int32, (own_cycles, 1, 1), 0)
    ) * n_cols + col_pos
    results = []
    candidate_measurement = measurement_rows[:, 0, :]
    cand_factor = prior_factor_rows[:, 0, :]
    for panel_number_index in range(panels):
        last_panel = panel_number_index + 1 == panels
        received_measurement, received_factor = (
            spread(candidate_measurement, "col", panel_number_index),
            spread(cand_factor, "col", panel_number_index),
        )
        measurement_gram = jnp.einsum(
            "nh,np->hp", received_measurement, received_measurement, precision=highest_precision
        )
        resident_rows = jnp.where(holder, received_factor, jnp.float32(0.0))
        measurement_gram, rows_of_panel = lax.psum((measurement_gram, resident_rows), "row")
        total_gram_matrix = measurement_gram + jnp.einsum(
            "nh,np->hp", rows_of_panel, rows_of_panel, precision=highest_precision
        )
        lower_cholesky = jnp.linalg.cholesky(total_gram_matrix)
        measurement_basis = jax.scipy.linalg.solve_triangular(
            lower_cholesky, received_measurement.T, lower=True
        ).T
        basis_row_block = jax.scipy.linalg.solve_triangular(
            lower_cholesky, rows_of_panel.T, lower=True
        ).T
        row_term = jnp.einsum(
            "yg,yfv->fgv", basis_row_block, prior_factor_rows, precision=highest_precision
        )
        padded_term = lax.dynamic_update_slice_in_dim(
            jnp.zeros((cycles, tile_size, tile_size), jnp.float32), row_term, first_cycle, 0
        )
        slice_portion = measurement_rows
        partial_sum_local = jnp.einsum(
            "yg,yfv->fgv", measurement_basis, slice_portion, precision=highest_precision
        )
        complete_coefficients = lax.psum(partial_sum_local + padded_term, "row")
        own_coeffs = lax.dynamic_slice_in_dim(complete_coefficients, first_cycle, own_cycles, 0)
        masked = jnp.where(block_ids >= panel_number_index, own_coeffs, jnp.float32(0.0))
        results.append(jnp.transpose(masked, (1, 0, 2)))
        if not last_panel:
            measurement_rows = measurement_rows - jnp.einsum(
                "ua,tah->uth", measurement_basis, complete_coefficients, precision=highest_precision
            )
            prior_factor_rows = prior_factor_rows - jnp.einsum(
                "ua,tah->uth", basis_row_block, own_coeffs, precision=highest_precision
            )
            candidate_measurement = measurement_rows[:, 0, :]
            cand_factor = prior_factor_rows[:, 0, :]
    return jnp.concatenate(results, axis=0)


def solution(mesh):
    in_specs = (P("row", None, "col"), P(None, "row", "col"))
    out_specs = P(None, "row", "col")
    return jax.shard_map(local, mesh=mesh, in_specs=in_specs, out_specs=out_specs, check_vma=False)
```

profile of v0, /device:TPU:32, one launch (start us, length us, event | category | flops | bytes accessed | tf_op | source)
XLA Modules:
  0.0 1248.7 jit_solution(6698926703810672527)
XLA Ops:
  6.5 0.0 all-reduce.17.cloned.1.call-start
  6.5 1.0 copy.5
  7.5 9.3 copy.3
  16.8 0.7 fusion.9
  17.5 1.9 fusion.5
  19.4 0.0 copy-start.3
  19.4 0.0 all-reduce.17.cloned.1.call-update
  19.4 0.0 all-reduce.21.cloned.1.call-start
  19.5 420.7 %all-reduce.17.cloned.1.call-done = (f32[1024,128]{1,0:T(8,128)}, f32[256,128]{1,0:T(8,128)}) async-done(((f32[1024,128]{1,0:T(8,128)}, f32[256,128]{1,0:T(8,128)}), (f32[1024,128]{1,0:T(8,128)}, f32[256,128]{1,0:T(8,128)})) %all-reduce.17.cloned.1.call-update) | async-done | bytes 655376 | tf_op jit(solution)/shard_map/psum | solution.py:11
  440.2 2.8 fusion.25
  443.0 0.7 broadcast_select_fusion.1
  443.7 0.0 all-reduce.21.cloned.1.call-update
  443.7 0.2 all-reduce.11.cloned.1.call-start
  444.0 67.2 %all-reduce.21.cloned.1.call-done = (f32[128,128]{0,1:T(8,128)}, f32[256,128]{1,0:T(8,128)}) async-done(((f32[128,128]{0,1:T(8,128)}, f32[256,128]{1,0:T(8,128)}), (f32[128,128]{0,1:T(8,128)}, f32[256,128]{1,0:T(8,128)})) %all-reduce.21.cloned.1.call-update) | async-done | bytes 196624 | tf_op jit(solution)/shard_map/psum | solution.py:42
  511.2 1.4 convolution_add_fusion.3
  512.5 0.1 copy.7
  512.6 11.7 cholesky.44
  524.4 0.6 compare_reduce_fusion.1
  525.0 0.7 fusion.13
  525.7 9.8 custom-call.10
  535.5 1.2 convolution_bitcast_fusion.3
  536.7 1.7 convolution_bitcast_fusion.1
  538.4 9.4 fusion.23
  547.8 0.1 copy.45
  547.9 0.0 copy-done.3
  547.9 0.3 fusion.3
  548.2 0.0 copy-start.2
  548.2 1.0 copy-done.2
  549.2 0.0 all-reduce.11.cloned.1.call-update
  549.2 0.3 all-reduce.15.cloned.1.call-start
  549.5 72.8 %all-reduce.11.cloned.1.call-done = f32[16,128,128]{2,1,0:T(8,128)} async-done(((f32[16,128,128]{2,1,0:T(8,128)}), f32[16,128,128]{2,1,0:T(8,128)}) %all-reduce.11.cloned.1.call-update) | async-done | bytes 1048592 | tf_op jit(solution)/shard_map/psum | solution.py:63
  622.3 1.3 convolution_subtract_fusion.1
  623.6 0.7 fusion.8
  624.3 11.8 convolution_subtract_fusion
  636.0 0.0 copy-start
  636.1 3.2 copy-done
  639.3 0.8 fusion.4
  640.1 0.0 all-reduce.15.cloned.1.call-update
  640.1 0.0 all-reduce.19.cloned.1.call-start
  640.1 419.9 %all-reduce.15.cloned.1.call-done = (f32[1024,128]{1,0:T(8,128)}, f32[256,128]{1,0:T(8,128)}) async-done(((f32[1024,128]{1,0:T(8,128)}, f32[256,128]{1,0:T(8,128)}), (f32[1024,128]{1,0:T(8,128)}, f32[256,128]{1,0:T(8,128)})) %all-reduce.15.cloned.1.call-update) | async-done | bytes 655376 | tf_op jit(solution)/shard_map/psum | solution.py:11
  1060.1 0.7 broadcast_select_fusion
  1060.8 2.8 fusion.26
  1063.6 0.0 all-reduce.19.cloned.1.call-update
  1063.6 0.0 all-reduce.13.cloned.1.call-start
  1063.7 67.4 %all-reduce.19.cloned.1.call-done = (f32[128,128]{0,1:T(8,128)}, f32[256,128]{1,0:T(8,128)}) async-done(((f32[128,128]{0,1:T(8,128)}, f32[256,128]{1,0:T(8,128)}), (f32[128,128]{0,1:T(8,128)}, f32[256,128]{1,0:T(8,128)})) %all-reduce.19.cloned.1.call-update) | async-done | bytes 196624 | tf_op jit(solution)/shard_map/psum | solution.py:42
  1131.1 1.4 convolution_add_fusion.2
  1132.4 0.1 copy.16
  1132.6 11.7 cholesky.55
  1144.3 0.6 compare_reduce_fusion
  1145.0 0.7 fusion.14
  1145.6 9.8 custom-call.12
  1155.4 1.2 convolution_bitcast_fusion.2
  1156.7 1.7 convolution_bitcast_fusion
  1158.3 7.1 fusion.27
  1165.4 0.1 copy.51
  1165.5 0.3 fusion.1
  1165.8 0.0 copy-start.1
  1165.8 1.0 copy-done.1
  1166.8 0.0 all-reduce.13.cloned.1.call-update
  1166.9 1.0 select_bitcast_fusion.1
  1167.9 72.1 %all-reduce.13.cloned.1.call-done = f32[16,128,128]{2,1,0:T(8,128)} async-done(((f32[16,128,128]{2,1,0:T(8,128)}), f32[16,128,128]{2,1,0:T(8,128)}) %all-reduce.13.cloned.1.call-update) | async-done | bytes 1048592 | tf_op jit(solution)/shard_map/psum | solution.py:63
  1239.9 1.0 select_bitcast_fusion
  1241.0 0.9 copy.22
  (6 shorter events, 0.1 us)
Async XLA Ops:
  6.5 433.7 %all-reduce.17.cloned.1.call-start = ((), (), s32[]{:S(2)}) async-start(), calls=%async_computation.3 | async-start | bytes 1310720 | tf_op jit(solution)/shard_map/psum | solution.py:11
  19.4 528.5 %copy-start.3 = (f32[256,2,128]{2,1,0:T(2,128)S(1)}, f32[256,2,128]{2,1,0:T(2,128)}, u32[]{:S(2)}) copy-start(f32[256,2,128]{2,1,0:T(2,128)} %param.8) | copy-start | bytes 786436
  19.4 491.7 %all-reduce.21.cloned.1.call-start = ((), (), s32[]{:S(2)}) async-start(), calls=%async_computation.5 | async-start | bytes 393216 | tf_op jit(solution)/shard_map/psum | solution.py:42
  443.7 178.5 %all-reduce.11.cloned.1.call-start = ((), (), s32[]{:S(2)}) async-start(), calls=%async_computation | async-start | bytes 2097152 | tf_op jit(solution)/shard_map/psum | solution.py:63
  548.2 1.0 copy-start.2
  549.2 510.9 %all-reduce.15.cloned.1.call-start = ((), (), s32[]{:S(2)}) async-start(), calls=%async_computation.2 | async-start | bytes 1310720 | tf_op jit(solution)/shard_map/psum | solution.py:11
  636.0 3.2 copy-start
  640.1 491.0 %all-reduce.19.cloned.1.call-start = ((), (), s32[]{:S(2)}) async-start(), calls=%async_computation.4 | async-start | bytes 393216 | tf_op jit(solution)/shard_map/psum | solution.py:42
  1063.6 176.3 %all-reduce.13.cloned.1.call-start = ((), (), s32[]{:S(2)}) async-start(), calls=%async_computation.1 | async-start | bytes 2097152 | tf_op jit(solution)/shard_map/psum | solution.py:63
  1165.8 1.0 copy-start.1
Sparse Core Ops, SparseCore 0:
  19.5 420.6 all-reduce.16
  443.8 67.2 all-reduce.20
  549.3 72.9 all-reduce.10
  640.2 419.8 all-reduce.14
  1063.7 67.3 all-reduce.18
  1167.0 72.9 all-reduce.12
where the time goes:
time: 1250 us
  waiting for transfers between devices  1120 us (90%)
  other arithmetic  53.1 us (4%)
  matrix products  44.3 us (4%)
  local copies, waits for them, and re-layouts  16.7 us (1%)
  between operations  13.7 us (1%)
    psum x2, waiting for transfers between devices, spread(): return lax.psum(jnp.where(mine, x, jnp.zeros_like(x)), axis)  841 us
    psum x2, waiting for transfers between devices, local(): complete_coefficients = lax.psum(partial_sum_local + padded_term, 'row')  145 us
    psum x2, waiting for transfers between devices, local(): lax.psum((measurement_gram, resident_rows), 'row')  135 us
  transfers between devices with their start and end apart: 6, of which 6 were waited for; matrix products, arithmetic and copies ran while one was open for 0% of the time, Pallas kernels for 0%

commit v1 on v0

v1 whole, which is shorter than its diff:
```python
import jax
import jax.numpy as jnp
from jax import lax
from jax.experimental import pallas as pl
from jax.experimental.pallas import tpu as pltpu
from jax.sharding import PartitionSpec as P

F32 = jnp.float32
BF16 = jnp.bfloat16
HIGHEST = lax.Precision.HIGHEST
ANY_CONTRACT = (((0,), (0,)), ((), ()))


def dot_tt(a, b):
    return lax.dot_general(a, b, ANY_CONTRACT, precision=HIGHEST, preferred_element_type=F32)


def dot(a, b):
    return jnp.dot(a, b, precision=HIGHEST, preferred_element_type=F32)


def split2(x):
    hi = x.astype(BF16)
    return hi, (x - hi.astype(F32)).astype(BF16)


def split3(x):
    one = x.astype(BF16).astype(F32)
    rest = x - one
    two = rest.astype(BF16).astype(F32)
    return one, two, rest - two


def eliminate(a_ref, u_ref, n):
    sub = lax.broadcasted_iota(jnp.int32, (8, n), 0)
    for k in range(n // 8):
        lo = 8 * k
        left = a_ref[lo : lo + 8, :n]
        right = a_ref[lo : lo + 8, n:]
        rl = [jnp.broadcast_to(left[p : p + 1, :], (8, n)) for p in range(8)]
        rr = [jnp.broadcast_to(right[p : p + 1, :], (8, n)) for p in range(8)]
        d = [
            [
                jnp.broadcast_to(left[p : p + 1, lo + q : lo + q + 1], (8, n)) if q >= p else None
                for q in range(8)
            ]
            for p in range(8)
        ]
        tl = tr = None
        for p in range(8):
            inv = 1.0 / d[p][p]
            rs = lax.rsqrt(d[p][p])
            rs = rs * (1.5 - 0.5 * d[p][p] * rs * rs)
            for q in range(p + 1, 8):
                factor = d[p][q] * inv
                for s in range(q, 8):
                    d[q][s] = d[q][s] - factor * d[p][s]
                rl[q] = rl[q] - factor * rl[p]
                rr[q] = rr[q] - factor * rr[p]
            a = rl[p] * rs
            b = rr[p] * rs
            tl = a if p == 0 else jnp.where(sub == p, a, tl)
            tr = b if p == 0 else jnp.where(sub == p, b, tr)
        u_ref[lo : lo + 8, :n] = tl
        u_ref[lo : lo + 8, n:] = tr
        if k + 1 < n // 8:
            t1, t2, t3 = split3(jnp.concatenate([tl, tr], axis=1))
            lhs = jnp.concatenate([t1[:, :n], t1[:, :n], t2[:, :n], t1[:, :n], t2[:, :n], t3[:, :n]], axis=0)
            rhs = jnp.concatenate([t1, t2, t1, t3, t2, t1], axis=0)
            update = lax.dot_general(
                lhs.astype(BF16), rhs.astype(BF16), ANY_CONTRACT, preferred_element_type=F32
            )
            a_ref[lo + 8 :, :] = a_ref[lo + 8 :, :] - update[lo + 8 :, :]


def factor_kernel(ids_ref, kept_ref, other_ref, w_ref, a_ref, u_ref):
    h = kept_ref.shape[0]
    first = ids_ref[1] == 0
    eye = (
        lax.broadcasted_iota(jnp.int32, (h, h), 0) == lax.broadcasted_iota(jnp.int32, (h, h), 1)
    ).astype(F32)
    top = jnp.where(first, kept_ref[...], other_ref[...])
    bottom = jnp.where(first, other_ref[:, h:], kept_ref[:, h:])
    a_ref[:, :h] = top[:, :h]
    a_ref[:, h:] = eye
    eliminate(a_ref, u_ref, h)
    w00 = u_ref[:, h:]
    w_ref[:h, :h] = w00
    w_ref[:h, h:] = jnp.zeros((h, h), F32)
    u01 = dot(w00, top[:, h:])
    a_ref[:, :h] = bottom - dot_tt(u01, u01)
    a_ref[:, h:] = eye
    x = dot_tt(u01, w00)
    eliminate(a_ref, u_ref, h)
    w11 = u_ref[:, h:]
    w_ref[h:, h:] = w11
    w_ref[h:, :h] = -dot(w11, x)


def split_kernel(obs_ref, hi_ref, lo_ref):
    for c in range(obs_ref.shape[1]):
        hi, lo = split2(obs_ref[:, c, :])
        hi_ref[c] = hi
        lo_ref[c] = lo


def panel_kernel(ids_ref, z_ref, hi_ref, lo_ref, keep_ref, send_ref, prior_ref, p_ref):
    pieces, panels, rows, width = z_ref.shape
    obs_rows = p_ref.shape[0] // pieces
    pri_rows = rows - obs_rows
    holder = ids_ref[0] == 0
    for i in range(pieces):
        for p in range(panels):
            p_ref[obs_rows * i : obs_rows * (i + 1), width * p : width * (p + 1)] = z_ref[i, p, :obs_rows, :]
            prior_ref[pri_rows * i : pri_rows * (i + 1), width * p : width * (p + 1)] = z_ref[i, p, obs_rows:, :]
    prior = jnp.where(holder, prior_ref[...], 0.0)
    panel = p_ref[...]
    turned = panel.T
    hi, lo = split2(turned)
    hi_ref[...] = hi
    lo_ref[...] = lo
    gram = dot(turned, panel) + dot_tt(prior, prior)
    half = gram.shape[0] // 2
    low = ids_ref[1] == 0
    keep_ref[...] = jnp.where(low, gram[:half], gram[half:])
    send_ref[...] = jnp.where(low, gram[half:], gram[:half])


def product_kernel(ids_ref, other, phi_ref, plo_ref, ahi_ref, alo_ref, out_ref):
    places, own, _, _ = out_ref.shape
    core = ids_ref[1]
    side = 1 - core if other else core
    phi = phi_ref[...]
    plo = plo_ref[...]

    def one(t, carry):
        z = t // own
        e = t % own
        c = (2 * z + side) * own + e
        hi = ahi_ref[c]
        lo = alo_ref[c]
        out_ref[z, e] = (
            jnp.dot(phi, hi, preferred_element_type=F32)
            + jnp.dot(phi, lo, preferred_element_type=F32)
            + jnp.dot(plo, hi, preferred_element_type=F32)
        )
        return carry

    lax.fori_loop(0, places * own, one, 0)


def combine_kernel(ids_ref, kept_ref, got_ref, *out_refs):
    z = ids_ref[0] // 2
    for k, out_ref in enumerate(out_refs):
        at = jnp.bitwise_xor(z, k)
        out_ref[...] = kept_ref[at] + got_ref[at]


def prior_kernel(panel_ref, own_ref, out_ref):
    for c in range(own_ref.shape[1]):
        out_ref[c] = dot_tt(panel_ref[...], own_ref[:, c, :])


def finish_kernel(n_col, ids_ref, w_ref, q_ref, a_ref, b_ref, c_ref, d_ref, out_ref):
    own, rows, width = q_ref.shape
    row_pos = ids_ref[0]
    col_pos = ids_ref[2]
    w = w_ref[...]
    for c in range(own):
        total = ((a_ref[c] + b_ref[c]) + (c_ref[c] + d_ref[c])) + q_ref[c]
        coeffs = dot(w, total)
        panel = lax.broadcasted_iota(jnp.int32, (rows, width), 0) // width
        block = (row_pos * own + c) * n_col + col_pos
        out_ref[:, c, :] = jnp.where(block >= panel, coeffs, 0.0)


def smem():
    return pl.BlockSpec(memory_space=pltpu.SMEM)


def vmem():
    return pl.BlockSpec(memory_space=pltpu.VMEM)


def call(kernel, name, out_shape, ids, *args, scratch=(), limit=48 << 20):
    return pl.pallas_call(
        kernel,
        out_shape=out_shape,
        in_specs=[smem()] + [vmem()] * len(args),
        out_specs=jax.tree.map(lambda _: vmem(), out_shape),
        scratch_shapes=list(scratch),
        compiler_params=pltpu.CompilerParams(vmem_limit_bytes=limit),
        name=name,
    )(ids, *args)


def struct(shape, dtype=F32):
    return jax.ShapeDtypeStruct(shape, dtype)


def local(observations, prior_rows):
    obs, cycles, width = observations.shape
    total_rows, own, _ = prior_rows.shape
    panels = total_rows // width
    n_row = lax.axis_size("row")
    n_col = lax.axis_size("col")
    plane = n_col // 2
    places = n_row // 2
    row_pos = lax.axis_index("row")
    col_pos = lax.axis_index("col")
    core = row_pos % 2
    ids = jnp.stack([row_pos, core, col_pos]).astype(jnp.int32)

    pieces = jnp.concatenate(
        [
            observations[:, 0, :].reshape(plane, obs // plane, width),
            prior_rows[:, 0, :].reshape(plane, total_rows // plane, width),
        ],
        axis=1,
    )
    planes = [[h * plane + i for i in range(plane)] for h in range(2)]
    got = lax.all_to_all(pieces, "col", 0, 0, tiled=True, axis_index_groups=planes)[:panels]
    far = lax.ppermute(got, "col", [(i, i + plane) for i in range(plane)])

    steps = 8
    ahi, alo = pl.pallas_call(
        split_kernel,
        grid=(steps,),
        in_specs=[pl.BlockSpec((obs // steps, cycles, width), lambda i: (i, 0, 0))],
        out_specs=[pl.BlockSpec((cycles, obs // steps, width), lambda i: (0, i, 0))] * 2,
        out_shape=[struct((cycles, obs, width), BF16)] * 2,
        name="split",
    )(observations)

    mine = jnp.where(col_pos >= plane, far, got)
    rows = mine.shape[1]
    spread = jnp.broadcast_to(mine[None], (plane, panels, rows, width))
    gathered = lax.all_to_all(spread, "col", 0, 0, tiled=True, axis_index_groups=planes)

    wide = panels * width
    phi, plo, gram_keep, gram_send, prior_panel = call(
        panel_kernel,
        "panel",
        [
            struct((wide, obs), BF16),
            struct((wide, obs), BF16),
            struct((wide // 2, wide)),
            struct((wide // 2, wide)),
            struct((total_rows, wide)),
        ],
        ids,
        gathered,
        scratch=[pltpu.VMEM((obs, wide), F32)],
    )

    def swap(x, k):
        return lax.ppermute(x, "row", [(r, r ^ k) for r in range(n_row)])

    gram = gram_keep + swap(gram_send, 1)

    def product(other):
        return call(
            lambda *refs: product_kernel(refs[0], other, *refs[1:]),
            "product_send" if other else "product_keep",
            struct((places, own, wide, width)),
            ids,
            phi,
            plo,
            ahi,
            alo,
        )

    sums_send = product(True)
    sums_got = swap(sums_send, 1)
    gram = gram + swap(gram, 2)
    gram = gram + swap(gram, 4)
    gram_other = swap(gram, 1)
    sums_keep = product(False)

    to = call(
        combine_kernel,
        "combine",
        [struct((own, wide, width))] * places,
        ids,
        sums_keep,
        sums_got,
    )
    came = [swap(to[k], 2 * k) for k in range(1, places)]

    w = call(
        factor_kernel,
        "factor",
        struct((wide, wide)),
        ids,
        gram,
        gram_other,
        scratch=[pltpu.VMEM((wide // 2, wide), F32)] * 2,
    )

    def hand(x, pairs):
        moved = lax.ppermute(x, "row", pairs)
        takes = jnp.zeros((), jnp.bool_)
        for _, dst in pairs:
            takes = takes | (row_pos == dst)
        return jnp.where(takes, moved, x)

    full = hand(prior_panel, [(0, 1)])
    part = lax.dynamic_slice_in_dim(full, core * (total_rows // 2), total_rows // 2, 0)
    part = hand(part, [(0, 4), (1, 5)])
    part = hand(part, [(0, 2), (1, 3), (4, 6), (5, 7)])
    rest = swap(part, 1)
    prior_full = jnp.where(
        core == 0, jnp.concatenate([part, rest], axis=0), jnp.concatenate([rest, part], axis=0)
    )
    q = pl.pallas_call(
        prior_kernel,
        out_shape=struct((own, wide, width)),
        name="prior",
    )(prior_full, prior_rows)

    return call(
        lambda *refs: finish_kernel(n_col, *refs),
        "finish",
        struct((total_rows, own, width)),
        ids,
        w,
        q,
        to[0],
        *came,
    )


def solution(mesh):
    in_specs = (P("row", None, "col"), P(None, "row", "col"))
    out_specs = P(None, "row", "col")
    return jax.shard_map(local, mesh=mesh, in_specs=in_specs, out_specs=out_specs, check_vma=False)
```

time: 1250 us -> 130 us (0.10)
  waiting for transfers between devices: 1120 us -> 10.9 us
  Pallas kernels: 0 us -> 60.7 us
  other arithmetic: 53.1 us -> 4.4 us
  matrix products: 44.3 us -> 0 us
  starting transfers between devices: 0.61 us -> 26.3 us
  blocking collectives: 0 us -> 19.8 us
  between operations: 13.7 us -> 0.2 us
    psum x6 -> x0, waiting for transfers between devices: 1120 us -> none  [the longest x2 841 us: spread(): return lax.psum(jnp.where(mine, x, jnp.zeros_like(x)), axis)]
    pallas_call x0 -> x8, Pallas kernels: none -> 60.7 us  [the longest x6 34.7 us: call(): pl.pallas_call(kernel, out_shape=out_shape, in_specs=[smem()] + [vmem()]...]
    another operation x10 -> x1, other arithmetic: 45.7 us -> 0.08 us  [local(): ids = jnp.stack([row_pos, core, col_pos]).astype(jnp.int32)]
    dot_general x10 -> x0, matrix products: 38.5 us -> none  [the longest x2 16.4 us: local(): jnp.einsum('yg,yfv->fgv', measurement_basis, slice_portion, precision=hig...]
    ppermute x0 -> x13, starting transfers between devices: none -> 22.6 us  [the longest x9 10.5 us: swap(): return lax.ppermute(x, 'row', [(r, r ^ k) for r in range(n_row)])]
    all_to_all x0 -> x1, blocking collectives: none -> 19.8 us  [local(): lax.all_to_all(pieces, 'col', 0, 0, tiled=True, axis_index_groups=planes)]
    unnamed x12 -> x2, local copies, waits for them, and re-layouts: 15.6 us -> 0.95 us
  transfers between devices with their start and end apart: 6 -> 14, of which waited for: 6 -> 5; matrix products, arithmetic and copies ran while one was open for 0% -> 3% of each run, Pallas kernels for 0% -> 38%
where the time goes in v1:
time: 130 us; the launch traced here: 128 us
  Pallas kernels  60.7 us (47%)
  starting transfers between devices  26.3 us (20%)
  blocking collectives  19.8 us (15%)
  waiting for transfers between devices  10.9 us (8%)
  local copies, waits for them, and re-layouts  5.74 us (4%)
  other arithmetic  4.4 us (3%)
    pallas_call x6, Pallas kernels, call(): pl.pallas_call(kernel, out_shape=out_shape, in_specs=[smem()] + [vmem()]...  34.7 us
    pallas_call x1, Pallas kernels, local(): pl.pallas_call(split_kernel, grid=(steps,), in_specs=[pl.BlockSpec((obs /...  23.5 us
    all_to_all x1, blocking collectives, local(): lax.all_to_all(pieces, 'col', 0, 0, tiled=True, axis_index_groups=planes)  19.8 us
    ppermute x9, starting transfers between devices, swap(): return lax.ppermute(x, 'row', [(r, r ^ k) for r in range(n_row)])  10.5 us
    ppermute x9, waiting for transfers between devices, swap(): return lax.ppermute(x, 'row', [(r, r ^ k) for r in range(n_row)])  8.85 us
    ppermute x1, starting transfers between devices, local(): far = lax.ppermute(got, 'col', [(i, i + plane) for i in range(plane)])  8.19 us
    ppermute x3, starting transfers between devices, hand(): moved = lax.ppermute(x, 'row', pairs)  3.99 us
    all_to_all x1, starting transfers between devices, local(): lax.all_to_all(spread, 'col', 0, 0, tiled=True, axis_index_groups=planes)  3.7 us
  transfers between devices with their start and end apart: 14, of which 5 were waited for; matrix products, arithmetic and copies ran while one was open for 3% of the time, Pallas kernels for 38%

profile of v1, /device:TPU:32, one launch (start us, length us, event | category | flops | bytes accessed | tf_op | source)
XLA Modules:
  0.0 128.1 jit_solution(5202154689531699954)
XLA Ops:
  0.0 1.0 slice.10
  1.0 2.5 %slice.9 = f32[1024,1,128]{2,1,0:T(1,128)S(1)} slice(f32[1024,16,128]{2,1,0:T(8,128)} %obs_ref.1), slice={[0:1024], [0:1], [0:128]} | slice | bytes 1048576 | tf_op jit(solution)/shard_map/slice | solution.py:216
  3.6 19.8 %all_to_all.10 = f32[16,80,128]{2,1,0:T(8,128)S(1)} all-to-all(f32[16,80,128]{2,1,0:T(8,128)S(1)} %pad_maximum_fusion), channel_id=1, replica_groups={{0,1,2,3,4,5,6,7,8,9,10,11,12,13,14,15},{16,17,18,19,20,21,22,23,24,25,..., dimensions={0} | all-to-all | bytes 1310720 | tf_op jit(solution)/shard_map/all_to_all | solution.py:222
  23.3 8.2 %collective-permute-start = (f32[2,80,128]{2,1,0:T(8,128)S(1)}, f32[2,80,128]{2,1,0:T(8,128)S(1)}, u32[]{:S(2)}, u32[]{:S(2)}) collective-permute-start(f32[2,80,128]{2,1,0:T(8,128)S(1)} %slice.12), channel_id=1, source_target_pairs={{0,16},{1,17},{2,18},{3,19},{4,20},{5,21},{6,22},{7,23},{8,24},{9,... | collective-permute-start | bytes 245768 | tf_op jit(solution)/shard_map/ppermute | solution.py:223
  31.5 2.0 %collective-permute-done = f32[2,80,128]{2,1,0:T(8,128)S(1)} collective-permute-done((f32[2,80,128]{2,1,0:T(8,128)S(1)}, f32[2,80,128]{2,1,0:T(8,128)S(1)}, u32[]{:S(2)}, u32[]{:S(2)}) %collective-permute-start) | collective-permute-done | bytes 81952 | tf_op jit(solution)/shard_map/ppermute | solution.py:223
  33.6 1.3 %broadcast_in_dim.2 = f32[16,2,80,128]{3,2,1,0:T(8,128)} broadcast(f32[2,80,128]{2,1,0:T(8,128)S(1)} %broadcast_select_fusion.2), dimensions={1,2,3} | broadcast | bytes 1392640 | tf_op jit(solution)/shard_map/broadcast_in_dim | solution.py:237
  34.9 3.7 %all-to-all-start.1 = ((f32[16,2,80,128]{3,2,1,0:T(8,128)}), f32[16,2,80,128]{3,2,1,0:T(8,128)S(1)}, u32[]{:S(2)}, u32[]{:S(2)}) async-start(f32[16,2,80,128]{3,2,1,0:T(8,128)} %broadcast_in_dim.2), calls=%async_computation.1 | async-start | bytes 2621440 | tf_op jit(solution)/shard_map/all_to_all | solution.py:238
  38.6 23.5 %split.1 = (bf16[16,1024,128]{2,1,0:T(8,128)(2,1)}, bf16[16,1024,128]{2,1,0:T(8,128)(2,1)}) custom-call(f32[1024,16,128]{2,1,0:T(8,128)} %obs_ref.1), custom_call_target="tpu_custom_call" | custom-call | tf_op jit(solution)/shard_map/split/pallas_call | solution.py:226
  62.1 0.1 pad_add_fusion.ids_ref.refs_0_
  62.2 0.0 all-to-all-done.1.z_ref
  62.2 2.6 %panel.1 = (bf16[256,1024]{1,0:T(8,128)(2,1)S(1)}, bf16[256,1024]{1,0:T(8,128)(2,1)S(1)}, f32[128,256]{1,0:T(8,128)S(1)}, f32[128,256]{1,0:T(8,128)}, f32[256,256]{1,0:T(8,128)}) custom-call(s32[3]{0:T(128)S(1)} %pad_add_fusion.ids_ref.refs_0_, f32[16,2,80,128]{3,2,1,0:T(8,128)S(1)} %all-to-all-done.1.z_ref), custom_call_target="tpu_custom_call" | custom-call | tf_op jit(solution)/shard_map/panel/pallas_call | solution.py:186
  64.7 8.1 %product_send.1 = f32[4,2,256,128]{3,2,1,0:T(8,128)S(1)} custom-call(s32[3]{0:T(128)S(1)} %pad_add_fusion.ids_ref.refs_0_, bf16[256,1024]{1,0:T(8,128)(2,1)S(1)} %get-tuple-element.19.refs_1_, bf16[256,1024]{1,0:T(8,128)(2,1)S(1)} %get-tuple-element.20.refs_2_, bf16[16,1024,128]{2,1,0:T(8,128)(2,1)} %get-tuple-element.21.refs_3_, ...), custom_call_target="tpu_custom_call" | custom-call | tf_op jit(solution)/shard_map/product_send/pallas_call | solution.py:186
  72.9 0.1 collective-permute-start.9
  73.0 1.4 %collective-permute-start.5 = (f32[256,256]{1,0:T(8,128)}, f32[256,256]{1,0:T(8,128)}, u32[]{:S(2)}, u32[]{:S(2)}) collective-permute-start(f32[256,256]{1,0:T(8,128)} %get-tuple-element.18), channel_id=1, source_target_pairs={{0,32},{1,33},{2,34},{3,35},{4,36},{5,37},{6,38},{7,39},{8,40},{9,... | collective-permute-start | bytes 786440 | tf_op jit(solution)/shard_map/ppermute | solution.py:301
  74.4 0.5 collective-permute-start.1
  74.9 1.2 collective-permute-done.1
  76.1 2.7 %collective-permute-start.2 = (f32[128,256]{1,0:T(8,128)S(1)}, f32[128,256]{1,0:T(8,128)}, u32[]{:S(2)}, u32[]{:S(2)}) collective-permute-start(f32[128,256]{1,0:T(8,128)S(1)} %add.17), channel_id=1, source_target_pairs={{0,64},{32,96},{64,0},{96,32},{128,192},{160,224},{192,128},{224,1... | collective-permute-start | bytes 393224 | tf_op jit(solution)/shard_map/ppermute | solution.py:257
  78.8 0.0 collective-permute-done.5
  78.8 1.0 dynamic-slice_select_fusion
  79.8 1.3 %collective-permute-start.6 = (f32[128,256]{1,0:T(8,128)S(1)}, f32[128,256]{1,0:T(8,128)}, u32[]{:S(2)}, u32[]{:S(2)}) collective-permute-start(f32[128,256]{1,0:T(8,128)S(1)} %dynamic-slice_select_fusion), channel_id=1, source_target_pairs={{0,128},{32,160},{1,129},{33,161},{2,130},{34,162},{3,131},{35,163... | collective-permute-start | bytes 393224 | tf_op jit(solution)/shard_map/ppermute | solution.py:301
  81.1 1.6 %collective-permute-done.2 = f32[128,256]{1,0:T(8,128)} collective-permute-done((f32[128,256]{1,0:T(8,128)S(1)}, f32[128,256]{1,0:T(8,128)}, u32[]{:S(2)}, u32[]{:S(2)}) %collective-permute-start.2) | collective-permute-done | bytes 131104 | tf_op jit(solution)/shard_map/ppermute | solution.py:257
  82.7 0.9 add.18
  83.6 0.9 collective-permute-start.3
  84.5 0.0 collective-permute-done.6
  84.5 0.7 broadcast_select_fusion
  85.2 1.3 collective-permute-start.7
  86.5 8.2 %product_keep.1.kept_ref = f32[4,2,256,128]{3,2,1,0:T(8,128)S(1)} custom-call(s32[3]{0:T(128)S(1)} %pad_add_fusion.ids_ref.refs_0_, bf16[256,1024]{1,0:T(8,128)(2,1)S(1)} %get-tuple-element.19.refs_1_, bf16[256,1024]{1,0:T(8,128)(2,1)S(1)} %get-tuple-element.20.refs_2_, bf16[16,1024,128]{2,1,0:T(8,128)(2,1)} %get-tuple-element.21.refs_3_, ...), custom_call_target="tpu_custom_call" | custom-call | tf_op jit(solution)/shard_map/product_keep/pallas_call | solution.py:186
  94.7 0.0 collective-permute-done.3
  94.7 0.9 add.19.kept_ref
  95.6 0.1 collective-permute-start.4
  95.7 0.0 collective-permute-done.9.got_ref
  95.7 0.7 combine.1
  96.4 2.7 %collective-permute-start.10 = (f32[2,256,128]{2,1,0:T(8,128)S(1)}, f32[2,256,128]{2,1,0:T(8,128)S(1)}, u32[]{:S(2)}, u32[]{:S(2)}) collective-permute-start(f32[2,256,128]{2,1,0:T(8,128)S(1)} %get-tuple-element.24), channel_id=1, source_target_pairs={{0,64},{32,96},{64,0},{96,32},{128,192},{160,224},{192,128},{224,1... | collective-permute-start | bytes 786440 | tf_op jit(solution)/shard_map/ppermute | solution.py:257
  99.1 3.2 %collective-permute-start.11 = (f32[2,256,128]{2,1,0:T(8,128)S(1)}, f32[2,256,128]{2,1,0:T(8,128)S(1)}, u32[]{:S(2)}, u32[]{:S(2)}) collective-permute-start(f32[2,256,128]{2,1,0:T(8,128)S(1)} %get-tuple-element.25), channel_id=1, source_target_pairs={{0,128},{32,160},{64,192},{96,224},{128,0},{160,32},{192,64},{224,... | collective-permute-start | bytes 786440 | tf_op jit(solution)/shard_map/ppermute | solution.py:257
  102.3 0.0 collective-permute-start.12
  102.3 0.0 collective-permute-done.7
  102.3 0.3 collective-permute-start.8
  102.6 0.0 collective-permute-done.4.other_ref
  102.6 13.2 %factor.1.refs_1_ = f32[256,256]{1,0:T(8,128)S(1)} custom-call(s32[3]{0:T(128)S(1)} %pad_add_fusion.ids_ref.refs_0_, f32[128,256]{1,0:T(8,128)S(1)} %add.19.kept_ref, f32[128,256]{1,0:T(8,128)S(1)} %collective-permute-done.4.other_ref), custom_call_target="tpu_custom_call" | custom-call | tf_op jit(solution)/shard_map/factor/pallas_call | solution.py:186
  115.9 0.0 collective-permute-done.8
  115.9 0.7 maximum_select_fusion.panel_ref
  116.6 2.5 %prior.1.refs_2_ = f32[2,256,128]{2,1,0:T(8,128)} custom-call(f32[256,256]{1,0:T(8,128)} %maximum_select_fusion.panel_ref, f32[256,2,128]{2,1,0:T(2,128)} %own_ref.1), custom_call_target="tpu_custom_call" | custom-call | tf_op jit(solution)/shard_map/prior/pallas_call | solution.py:315
  119.1 0.0 collective-permute-done.10.refs_4_
  119.1 1.2 collective-permute-done.11.refs_5_
  120.2 4.9 %collective-permute-done.12.refs_6_ = f32[2,256,128]{2,1,0:T(8,128)S(1)} collective-permute-done((f32[2,256,128]{2,1,0:T(8,128)S(1)}, f32[2,256,128]{2,1,0:T(8,128)S(1)}, u32[]{:S(2)}, u32[]{:S(2)}) %collective-permute-start.12) | collective-permute-done | bytes 262176 | tf_op jit(solution)/shard_map/ppermute | solution.py:257
  125.1 0.0 copy-start
  125.1 0.9 copy-done
  126.1 2.0 %finish.1 = f32[256,2,128]{2,1,0:T(2,128)} custom-call(s32[3]{0:T(128)S(1)} %pad_add_fusion.ids_ref.refs_0_, f32[256,256]{1,0:T(8,128)S(1)} %factor.1.refs_1_, f32[2,256,128]{2,1,0:T(8,128)S(1)} %copy-done, f32[2,256,128]{2,1,0:T(8,128)S(1)} %get-tuple-element.23.refs_3_, f32[2,256,128]{2,1,0:T(8,128)S(1)} %collective-permute-done.10.refs_4_, ...), custom_call_target="tpu_custom_call" | custom-call | tf_op jit(solution)/shard_map/finish/pallas_call | solution.py:186
  (5 shorter events, 0.1 us)
Async XLA Ops:
  23.3 10.2 %collective-permute-start = (f32[2,80,128]{2,1,0:T(8,128)S(1)}, f32[2,80,128]{2,1,0:T(8,128)S(1)}, u32[]{:S(2)}, u32[]{:S(2)}) collective-permute-start(f32[2,80,128]{2,1,0:T(8,128)S(1)} %slice.12), channel_id=1, source_target_pairs={{0,16},{1,17},{2,18},{3,19},{4,20},{5,21},{6,22},{7,23},{8,24},{9,... | collective-permute-start | bytes 245768 | tf_op jit(solution)/shard_map/ppermute | solution.py:223
  34.9 27.3 %all-to-all-start.1 = ((f32[16,2,80,128]{3,2,1,0:T(8,128)}), f32[16,2,80,128]{3,2,1,0:T(8,128)S(1)}, u32[]{:S(2)}, u32[]{:S(2)}) async-start(f32[16,2,80,128]{3,2,1,0:T(8,128)} %broadcast_in_dim.2), calls=%async_computation.1 | async-start | bytes 2621440 | tf_op jit(solution)/shard_map/all_to_all | solution.py:238
  72.9 22.8 %collective-permute-start.9 = (f32[4,2,256,128]{3,2,1,0:T(8,128)S(1)}, f32[4,2,256,128]{3,2,1,0:T(8,128)S(1)}, u32[]{:S(2)}, u32[]{:S(2)}) collective-permute-start(f32[4,2,256,128]{3,2,1,0:T(8,128)S(1)} %product_send.1), channel_id=1, source_target_pairs={{0,32},{32,0},{64,96},{96,64},{128,160},{160,128},{192,224},{224,1... | collective-permute-start | bytes 3145736 | tf_op jit(solution)/shard_map/ppermute | solution.py:257
  73.0 5.8 %collective-permute-start.5 = (f32[256,256]{1,0:T(8,128)}, f32[256,256]{1,0:T(8,128)}, u32[]{:S(2)}, u32[]{:S(2)}) collective-permute-start(f32[256,256]{1,0:T(8,128)} %get-tuple-element.18), channel_id=1, source_target_pairs={{0,32},{1,33},{2,34},{3,35},{4,36},{5,37},{6,38},{7,39},{8,40},{9,... | collective-permute-start | bytes 786440 | tf_op jit(solution)/shard_map/ppermute | solution.py:301
  74.4 1.7 %collective-permute-start.1 = (f32[128,256]{1,0:T(8,128)}, f32[128,256]{1,0:T(8,128)S(1)}, u32[]{:S(2)}, u32[]{:S(2)}) collective-permute-start(f32[128,256]{1,0:T(8,128)} %get-tuple-element.17), channel_id=1, source_target_pairs={{0,32},{32,0},{64,96},{96,64},{128,160},{160,128},{192,224},{224,1... | collective-permute-start | bytes 393224 | tf_op jit(solution)/shard_map/ppermute | solution.py:257
  76.1 6.6 %collective-permute-start.2 = (f32[128,256]{1,0:T(8,128)S(1)}, f32[128,256]{1,0:T(8,128)}, u32[]{:S(2)}, u32[]{:S(2)}) collective-permute-start(f32[128,256]{1,0:T(8,128)S(1)} %add.17), channel_id=1, source_target_pairs={{0,64},{32,96},{64,0},{96,32},{128,192},{160,224},{192,128},{224,1... | collective-permute-start | bytes 393224 | tf_op jit(solution)/shard_map/ppermute | solution.py:257
  79.8 4.8 %collective-permute-start.6 = (f32[128,256]{1,0:T(8,128)S(1)}, f32[128,256]{1,0:T(8,128)}, u32[]{:S(2)}, u32[]{:S(2)}) collective-permute-start(f32[128,256]{1,0:T(8,128)S(1)} %dynamic-slice_select_fusion), channel_id=1, source_target_pairs={{0,128},{32,160},{1,129},{33,161},{2,130},{34,162},{3,131},{35,163... | collective-permute-start | bytes 393224 | tf_op jit(solution)/shard_map/ppermute | solution.py:301
  83.6 11.0 %collective-permute-start.3 = (f32[128,256]{1,0:T(8,128)S(1)}, f32[128,256]{1,0:T(8,128)}, u32[]{:S(2)}, u32[]{:S(2)}) collective-permute-start(f32[128,256]{1,0:T(8,128)S(1)} %add.18), channel_id=1, source_target_pairs={{0,128},{32,160},{64,192},{96,224},{128,0},{160,32},{192,64},{224,... | collective-permute-start | bytes 393224 | tf_op jit(solution)/shard_map/ppermute | solution.py:257
  85.2 17.1 %collective-permute-start.7 = (f32[128,256]{1,0:T(8,128)}, f32[128,256]{1,0:T(8,128)S(1)}, u32[]{:S(2)}, u32[]{:S(2)}) collective-permute-start(f32[128,256]{1,0:T(8,128)} %broadcast_select_fusion), channel_id=1, source_target_pairs={{0,64},{32,96},{128,192},{160,224},{1,65},{33,97},{129,193},{161,2... | collective-permute-start | bytes 393224 | tf_op jit(solution)/shard_map/ppermute | solution.py:301
  95.6 7.0 %collective-permute-start.4 = (f32[128,256]{1,0:T(8,128)S(1)}, f32[128,256]{1,0:T(8,128)S(1)}, u32[]{:S(2)}, u32[]{:S(2)}) collective-permute-start(f32[128,256]{1,0:T(8,128)S(1)} %add.19.kept_ref), channel_id=1, source_target_pairs={{0,32},{32,0},{64,96},{96,64},{128,160},{160,128},{192,224},{224,1... | collective-permute-start | bytes 393224 | tf_op jit(solution)/shard_map/ppermute | solution.py:257
  96.4 22.7 %collective-permute-start.10 = (f32[2,256,128]{2,1,0:T(8,128)S(1)}, f32[2,256,128]{2,1,0:T(8,128)S(1)}, u32[]{:S(2)}, u32[]{:S(2)}) collective-permute-start(f32[2,256,128]{2,1,0:T(8,128)S(1)} %get-tuple-element.24), channel_id=1, source_target_pairs={{0,64},{32,96},{64,0},{96,32},{128,192},{160,224},{192,128},{224,1... | collective-permute-start | bytes 786440 | tf_op jit(solution)/shard_map/ppermute | solution.py:257
  99.1 21.1 %collective-permute-start.11 = (f32[2,256,128]{2,1,0:T(8,128)S(1)}, f32[2,256,128]{2,1,0:T(8,128)S(1)}, u32[]{:S(2)}, u32[]{:S(2)}) collective-permute-start(f32[2,256,128]{2,1,0:T(8,128)S(1)} %get-tuple-element.25), channel_id=1, source_target_pairs={{0,128},{32,160},{64,192},{96,224},{128,0},{160,32},{192,64},{224,... | collective-permute-start | bytes 786440 | tf_op jit(solution)/shard_map/ppermute | solution.py:257
  102.3 22.8 %collective-permute-start.12 = (f32[2,256,128]{2,1,0:T(8,128)S(1)}, f32[2,256,128]{2,1,0:T(8,128)S(1)}, u32[]{:S(2)}, u32[]{:S(2)}) collective-permute-start(f32[2,256,128]{2,1,0:T(8,128)S(1)} %get-tuple-element.26), channel_id=1, source_target_pairs={{0,192},{32,224},{64,128},{96,160},{128,64},{160,96},{192,0},{224,... | collective-permute-start | bytes 786440 | tf_op jit(solution)/shard_map/ppermute | solution.py:257
  102.3 13.5 %collective-permute-start.8 = (f32[128,256]{1,0:T(8,128)S(1)}, f32[128,256]{1,0:T(8,128)S(1)}, u32[]{:S(2)}, u32[]{:S(2)}) collective-permute-start(f32[128,256]{1,0:T(8,128)S(1)} %broadcast_select_fusion.1), channel_id=1, source_target_pairs={{0,32},{32,0},{64,96},{96,64},{128,160},{160,128},{192,224},{224,1... | collective-permute-start | bytes 393224 | tf_op jit(solution)/shard_map/ppermute | solution.py:257
  125.1 0.9 copy-start

commit v2 on v1

v2 whole, which is shorter than its diff:
```python
import jax
import jax.numpy as jnp
from jax import lax
from jax.experimental import pallas as pl
from jax.experimental.pallas import tpu as pltpu
from jax.sharding import PartitionSpec as P

F32 = jnp.float32
BF16 = jnp.bfloat16
HIGHEST = lax.Precision.HIGHEST
ANY_CONTRACT = (((0,), (0,)), ((), ()))


def dot_tt(a, b):
    return lax.dot_general(a, b, ANY_CONTRACT, precision=HIGHEST, preferred_element_type=F32)


def dot(a, b):
    return jnp.dot(a, b, precision=HIGHEST, preferred_element_type=F32)


def split2(x):
    hi = x.astype(BF16)
    return hi, (x - hi.astype(F32)).astype(BF16)


def split3(x):
    one = x.astype(BF16).astype(F32)
    rest = x - one
    two = rest.astype(BF16).astype(F32)
    return one, two, rest - two


def eliminate(a_ref, u_ref, n):
    sub = lax.broadcasted_iota(jnp.int32, (8, n), 0)
    for k in range(n // 8):
        lo = 8 * k
        left = a_ref[lo : lo + 8, :n]
        right = a_ref[lo : lo + 8, n:]
        rl = [jnp.broadcast_to(left[p : p + 1, :], (8, n)) for p in range(8)]
        rr = [jnp.broadcast_to(right[p : p + 1, :], (8, n)) for p in range(8)]
        d = [
            [
                jnp.broadcast_to(left[p : p + 1, lo + q : lo + q + 1], (8, n)) if q >= p else None
                for q in range(8)
            ]
            for p in range(8)
        ]
        tl = tr = None
        for p in range(8):
            inv = 1.0 / d[p][p]
            rs = lax.rsqrt(d[p][p])
            rs = rs * (1.5 - 0.5 * d[p][p] * rs * rs)
            for q in range(p + 1, 8):
                factor = d[p][q] * inv
                for s in range(q, 8):
                    d[q][s] = d[q][s] - factor * d[p][s]
                rl[q] = rl[q] - factor * rl[p]
                rr[q] = rr[q] - factor * rr[p]
            a = rl[p] * rs
            b = rr[p] * rs
            tl = a if p == 0 else jnp.where(sub == p, a, tl)
            tr = b if p == 0 else jnp.where(sub == p, b, tr)
        u_ref[lo : lo + 8, :n] = tl
        u_ref[lo : lo + 8, n:] = tr
        if k + 1 < n // 8:
            t1, t2, t3 = split3(jnp.concatenate([tl, tr], axis=1))
            lhs = jnp.concatenate([t1[:, :n], t1[:, :n], t2[:, :n], t1[:, :n], t2[:, :n], t3[:, :n]], axis=0)
            rhs = jnp.concatenate([t1, t2, t1, t3, t2, t1], axis=0)
            update = lax.dot_general(
                lhs.astype(BF16), rhs.astype(BF16), ANY_CONTRACT, preferred_element_type=F32
            )
            a_ref[lo + 8 :, :] = a_ref[lo + 8 :, :] - update[lo + 8 :, :]


def blocks(rows):
    h = rows.shape[1] // 2
    top = dot_tt(rows[:, :h], rows)
    return jnp.concatenate([top[:, :h], top[:, h:], dot_tt(rows[:, h:], rows[:, h:])], axis=0)


def factor_kernel(ids_ref, kept_ref, other_ref, w_ref, a_ref, u_ref):
    half, h = kept_ref.shape
    low = ids_ref[1] == 0
    kept = kept_ref[...]
    other = other_ref[...]
    stack = jnp.concatenate([jnp.where(low, kept, other), jnp.where(low, other, kept)], axis=0)
    eye = (
        lax.broadcasted_iota(jnp.int32, (h, h), 0) == lax.broadcasted_iota(jnp.int32, (h, h), 1)
    ).astype(F32)
    a_ref[:, :h] = stack[:h]
    a_ref[:, h:] = eye
    eliminate(a_ref, u_ref, h)
    w00 = u_ref[:, h:]
    w_ref[:h, :h] = w00
    w_ref[:h, h:] = jnp.zeros((h, h), F32)
    u01 = dot(w00, stack[h : 2 * h])
    a_ref[:, :h] = stack[2 * h :] - dot_tt(u01, u01)
    a_ref[:, h:] = eye
    x = dot_tt(u01, w00)
    eliminate(a_ref, u_ref, h)
    w11 = u_ref[:, h:]
    w_ref[h:, h:] = w11
    w_ref[h:, :h] = -dot(w11, x)


def split_kernel(ids_ref, obs_ref, hi_ref, lo_ref, next_ref, buf, sems):
    rows, cycles, width = obs_ref.shape
    own = cycles // (2 * hi_ref.shape[1])
    core = ids_ref[1]
    copies = [pltpu.make_async_copy(obs_ref.at[:, c, :], buf.at[c], sems.at[c]) for c in range(cycles)]
    for copy in copies:
        copy.start()
    for i in range(3):
        next_ref[i] = ids_ref[i]
    for c, copy in enumerate(copies):
        copy.wait()
        place, at = divmod(c, own)
        z, side = divmod(place, 2)
        hi, lo = split2(buf[c].T)
        kept = jnp.where(core == side, 1, 0)
        hi_ref[kept, z, at * width : (at + 1) * width, :] = hi
        lo_ref[kept, z, at * width : (at + 1) * width, :] = lo


def prior_kernel(own_ref, got_ref, *refs):
    *columns, out_ref = refs
    panel = own_ref[...] + got_ref[...]
    for z, ref in enumerate(columns):
        width = ref.shape[2]
        for e in range(ref.shape[1]):
            out_ref[z, e * width : (e + 1) * width, :] = dot_tt(ref[:, e, :], panel)


def pieces_kernel(obs_ref, pri_ref, out_ref, sem, psem):
    pieces, rows, width = out_ref.shape
    n = obs_ref.shape[0] // pieces
    copies = []
    for i in range(pieces):
        copies.append(
            pltpu.make_async_copy(obs_ref.at[n * i : n * (i + 1), 0, :], out_ref.at[i, :n, :], sem.at[i])
        )
        m = rows - n
        copies.append(
            pltpu.make_async_copy(pri_ref.at[m * i : m * (i + 1), 0, :], out_ref.at[i, n:, :], psem.at[i])
        )
    for copy in copies:
        copy.start()
    for copy in copies:
        copy.wait()


def assembled(z_ref, n):
    pieces, panels, rows, width = z_ref.shape
    return [
        jnp.concatenate([z_ref[:, p, a:b, :].reshape(pieces * (b - a), width) for p in range(panels)], axis=1)
        for a, b in ((0, n), (n, rows))
    ]


def gram_kernel(n, ids_ref, z_ref, keep_ref, send_ref, prior_ref):
    rows, prior = assembled(z_ref, n)
    prior_ref[...] = prior
    stack = blocks(jnp.concatenate([rows, prior], axis=0))
    half = stack.shape[0] // 2
    low = ids_ref[1] == 0
    keep_ref[...] = jnp.where(low, stack[:half], stack[half:])
    send_ref[...] = jnp.where(low, stack[half:], stack[:half])


def panel_kernel(n, ids_ref, z_ref, hi_ref, lo_ref):
    hi_ref[...], lo_ref[...] = split2(assembled(z_ref, n)[0])


def product_kernel(ids_ref, phi_ref, plo_ref, ahi_ref, alo_ref, send_ref, keep_ref):
    for side, out_ref in enumerate((send_ref, keep_ref)):
        for z in range(out_ref.shape[0]):
            out_ref[z] = (
                jnp.dot(ahi_ref[side, z], phi_ref[...], preferred_element_type=F32)
                + jnp.dot(ahi_ref[side, z], plo_ref[...], preferred_element_type=F32)
                + jnp.dot(alo_ref[side, z], phi_ref[...], preferred_element_type=F32)
            )


def combine_kernel(ids_ref, kept_ref, got_ref, prior_ref, *out_refs):
    z = ids_ref[0] // 2
    for k, out_ref in enumerate(out_refs):
        at = jnp.bitwise_xor(z, k)
        out_ref[...] = kept_ref[at] + got_ref[at] + prior_ref[at]


def finish_kernel(n_col, ids_ref, w_ref, *refs):
    out_ref = refs[-1]
    rows, own, width = out_ref.shape
    part = [ref[...] for ref in refs[:-1]]
    while len(part) > 1:
        part = [a + b for a, b in zip(part[::2], part[1::2])] + part[len(part) // 2 * 2 :]
    coeffs = lax.dot_general(
        w_ref[...], part[0], (((1,), (1,)), ((), ())), precision=HIGHEST, preferred_element_type=F32
    )
    panel = lax.broadcasted_iota(jnp.int32, (rows, width), 0) // width
    for c in range(own):
        block = (ids_ref[0] * own + c) * n_col + ids_ref[2]
        out_ref[:, c, :] = jnp.where(block >= panel, coeffs[:, c * width : (c + 1) * width], 0.0)


def smem():
    return pl.BlockSpec(memory_space=pltpu.SMEM)


def vmem():
    return pl.BlockSpec(memory_space=pltpu.VMEM)


def anywhere():
    return pl.BlockSpec(memory_space=pltpu.HBM)


def call(kernel, name, us, out_shape, *args, ids=None, specs=None, outs=None, scratch=(), limit=32 << 20):
    specs = specs or [vmem()] * len(args)
    first = () if ids is None else (ids,)
    return pl.pallas_call(
        kernel,
        out_shape=out_shape,
        in_specs=[smem()] * len(first) + specs,
        out_specs=outs or jax.tree.map(lambda _: vmem(), out_shape),
        scratch_shapes=list(scratch),
        compiler_params=pltpu.CompilerParams(vmem_limit_bytes=limit),
        cost_estimate=pl.CostEstimate(flops=0, bytes_accessed=int(us * 3.6e6), transcendentals=0),
        name=name,
    )(*first, *args)


def gated(x, after):
    return lax.optimization_barrier((x, after))[0]


def inhbm(x):
    return pltpu.with_memory_space_constraint(x, pltpu.HBM)


def held(shape, dtype):
    return pltpu.VMEM(shape, dtype)


def struct(shape, dtype=F32):
    return jax.ShapeDtypeStruct(shape, dtype)


def local(observations, prior_rows):
    obs, cycles, width = observations.shape
    total_rows, own, _ = prior_rows.shape
    panels = total_rows // width
    n_row = lax.axis_size("row")
    n_col = lax.axis_size("col")
    plane = n_col // 2
    places = n_row // 2
    wide = panels * width
    pairs = cycles // own
    row_pos = lax.axis_index("row")
    col_pos = lax.axis_index("col")
    ids = jnp.stack([row_pos, row_pos % 2, col_pos]).astype(jnp.int32)
    planes = [[h * plane + i for i in range(plane)] for h in range(2)]

    def exchange(x):
        return lax.all_to_all(x, "col", 0, 0, tiled=True, axis_index_groups=planes)

    def share(x):
        return exchange(jnp.broadcast_to(x[None], (plane,) + x.shape))

    def swap(x, k):
        return lax.ppermute(x, "row", [(r, r ^ k) for r in range(n_row)])

    def across(x):
        far = lax.ppermute(x, "col", [(i, i + plane) for i in range(plane)])
        return jnp.where(col_pos >= plane, far, x)

    each = obs // plane
    pieces = call(
        pieces_kernel,
        "pieces",
        2,
        struct((plane, each + total_rows // plane, width)),
        inhbm(observations),
        inhbm(prior_rows),
        specs=[anywhere()] * 2,
        scratch=[pltpu.SemaphoreType.DMA((plane,))] * 2,
    )
    got = exchange(pieces)[:panels]
    holder = 2
    moved = [
        lax.ppermute(
            got[:, each:, :],
            ("row", "col"),
            [(c, holder * n_col + c + h * plane) for c in range(plane)],
        )
        for h in range(2)
    ]
    rows = across(got[:, :each, :])
    prior = jnp.where(ids[0] == holder, moved[0] + moved[1], 0.0)
    ids, full = lax.optimization_barrier((ids, jnp.concatenate([rows, prior], axis=1)))
    gathered = share(full)
    ahi, alo, ids = call(
        split_kernel,
        "split",
        6,
        [held((2, places, own * width, obs), BF16)] * 2 + [struct((3,), jnp.int32)],
        inhbm(observations),
        ids=ids,
        specs=[anywhere()],
        outs=[vmem(), vmem(), smem()],
        scratch=[pltpu.VMEM((cycles, obs, width), F32), pltpu.SemaphoreType.DMA((cycles,))],
    )
    columns = [
        prior_rows
        if 2 * z == holder
        else lax.ppermute(prior_rows, "row", [(2 * z + core, holder + core) for core in range(2)])
        for z in range(places)
    ]

    gathered, ids, *columns = lax.optimization_barrier((gathered, ids, *columns))
    gram_keep, gram_send, prior_panel = call(
        lambda *refs: gram_kernel(each, *refs),
        "gram",
        1.5,
        [struct((3 * width // 2, width))] * 2 + [struct((total_rows, wide))],
        gathered,
        ids=ids,
    )
    gram_got = swap(gram_send, 1)
    panel = call(
        lambda *refs: panel_kernel(each, *refs),
        "panel",
        0.4,
        [struct((obs, wide), BF16)] * 2,
        gathered,
        ids=gated(ids, gram_send),
    )

    prior_sums = call(
        prior_kernel,
        "prior",
        2,
        struct((places, own * width, wide)),
        prior_panel,
        lax.ppermute(prior_panel, "row", [(holder, holder + 1)]),
        *columns,
    )

    gram = gram_keep + gram_got
    gram_far = [swap(gram, 2 * k) for k in range(1, places)]
    sums_send, sums_keep = call(
        product_kernel,
        "product",
        7,
        [struct((places, own * width, wide))] * 2,
        *panel,
        pltpu.with_memory_space_constraint(ahi, pltpu.VMEM),
        pltpu.with_memory_space_constraint(alo, pltpu.VMEM),
        ids=gated(ids, gram),
    )
    sums_got = swap(sums_send, 1)
    gram = (gram + gram_far[0]) + (gram_far[1] + gram_far[2])
    gram_other = swap(gram, 1)
    to = call(
        combine_kernel,
        "combine",
        0.6,
        [struct((own * width, wide))] * places,
        sums_keep,
        sums_got,
        prior_sums,
        ids=ids,
    )
    came = [swap(to[k], 2 * k) for k in range(1, places)]
    w = call(
        factor_kernel,
        "factor",
        13,
        struct((wide, wide)),
        gram,
        gram_other,
        ids=ids,
        scratch=[pltpu.VMEM((wide // 2, wide), F32)] * 2,
    )
    return call(
        lambda *refs: finish_kernel(n_col, *refs),
        "finish",
        2,
        struct((total_rows, own, width)),
        w,
        to[0],
        *came,
        ids=ids,
    )


def solution(mesh):
    in_specs = (P("row", None, "col"), P(None, "row", "col"))
    out_specs = P(None, "row", "col")
    return jax.shard_map(local, mesh=mesh, in_specs=in_specs, out_specs=out_specs, check_vma=False)
```

time: 130 us -> 107 us (0.82); the launches traced: 128 us -> 107 us
  Pallas kernels: 60.7 us -> 31.5 us
  waiting for transfers between devices: 10.9 us -> 32 us
  blocking collectives: 19.8 us -> 0 us
  starting transfers between devices: 26.3 us -> 33.5 us
  other arithmetic: 4.4 us -> 0.13 us
  local copies, waits for them, and re-layouts: 5.74 us -> 9.59 us
    pallas_call x8 -> x9, Pallas kernels: 60.7 us -> 31.5 us  [call(): pl.pallas_call(kernel, out_shape=out_shape, in_specs=[smem()] * len(first...]
    all_to_all x1 -> x0, blocking collectives: 19.8 us -> none  [local(): lax.all_to_all(pieces, 'col', 0, 0, tiled=True, axis_index_groups=planes)]
    all_to_all x1 -> x2, waiting for transfers between devices: 0.01 us -> 17.4 us  [exchange(): return lax.all_to_all(x, 'col', 0, 0, tiled=True, axis_index_groups=planes)]
    unnamed x2 -> x10, local copies, waits for them, and re-layouts: 0.95 us -> 8.35 us
    all_to_all x1 -> x2, starting transfers between devices: 3.7 us -> 10.9 us  [exchange(): return lax.all_to_all(x, 'col', 0, 0, tiled=True, axis_index_groups=planes)]
    ppermute x9, starting transfers between devices: 10.5 us -> 6.32 us  [swap(): return lax.ppermute(x, 'row', [(r, r ^ k) for r in range(n_row)])]
    ppermute x4 -> x7, starting transfers between devices: 12.2 us -> 16.3 us  [the longest x1 8.19 us: across(): far = lax.ppermute(x, 'col', [(i, i + plane) for i in range(plane)])]
    slice x3 -> x2, local copies, waits for them, and re-layouts: 3.51 us -> 0.01 us  [the longest x1 0.01 us: local(): rows = across(got[:, :each, :])]
  transfers between devices with their start and end apart: 14 -> 18, of which waited for: 5 -> 9; matrix products, arithmetic and copies ran while one was open for 3% -> 0% of each run, Pallas kernels for 38% -> 20%
where the time goes in v2:
time: 107 us
  starting transfers between devices  33.5 us (31%)
  waiting for transfers between devices  32 us (30%)
  Pallas kernels  31.5 us (29%)
  local copies, waits for them, and re-layouts  9.59 us (9%)
    pallas_call x9, Pallas kernels, call(): pl.pallas_call(kernel, out_shape=out_shape, in_specs=[smem()] * len(first...  31.5 us
    all_to_all x2, waiting for transfers between devices, exchange(): return lax.all_to_all(x, 'col', 0, 0, tiled=True, axis_index_groups=planes)  17.4 us
    ppermute x9, waiting for transfers between devices, swap(): return lax.ppermute(x, 'row', [(r, r ^ k) for r in range(n_row)])  12.1 us
    all_to_all x2, starting transfers between devices, exchange(): return lax.all_to_all(x, 'col', 0, 0, tiled=True, axis_index_groups=planes)  10.9 us
    unnamed x10, local copies, waits for them, and re-layouts  8.35 us
    ppermute x1, starting transfers between devices, across(): far = lax.ppermute(x, 'col', [(i, i + plane) for i in range(plane)])  8.19 us
    ppermute x9, starting transfers between devices, swap(): return lax.ppermute(x, 'row', [(r, r ^ k) for r in range(n_row)])  6.32 us
    ppermute x3, starting transfers between devices, local(): lax.ppermute(prior_rows, 'row', [(2 * z + core, holder + core) for core i...  3.88 us
  transfers between devices with their start and end apart: 18, of which 9 were waited for; matrix products, arithmetic and copies ran while one was open for 0% of the time, Pallas kernels for 20%

profile of v2, /device:TPU:32, one launch (start us, length us, event | category | flops | bytes accessed | tf_op | source)
XLA Modules:
  0.0 106.9 jit_solution(11749196961857493817)
XLA Ops:
  0.0 2.3 %pieces.1 = f32[16,80,128]{2,1,0:T(8,128)} custom-call(f32[1024,16,128]{2,1,0:T(8,128)} %obs_ref.3, f32[256,2,128]{2,1,0:T(2,128)} %refs_1_), custom_call_target="tpu_custom_call" | custom-call | bytes 7200000 | tf_op jit(solution)/shard_map/pieces/pallas_call | solution.py:222
  2.3 0.0 copy-start.4
  2.3 7.2 %all-to-all-start = ((f32[16,80,128]{2,1,0:T(8,128)}), f32[16,80,128]{2,1,0:T(8,128)S(1)}, u32[]{:S(2)}, u32[]{:S(2)}) async-start(f32[16,80,128]{2,1,0:T(8,128)} %pieces.1), calls=%async_computation | async-start | bytes 1310720 | tf_op jit(solution)/shard_map/all_to_all | solution.py:266
  9.5 12.9 %all-to-all-done = f32[16,80,128]{2,1,0:T(8,128)S(1)} async-done(((f32[16,80,128]{2,1,0:T(8,128)}), f32[16,80,128]{2,1,0:T(8,128)S(1)}, u32[]{:S(2)}, u32[]{:S(2)}) %all-to-all-start) | async-done | bytes 655392 | tf_op jit(solution)/shard_map/all_to_all | solution.py:266
  22.4 0.7 collective-permute-start.2
  23.1 1.3 %collective-permute-start.1 = (f32[2,16,128]{2,1,0:T(8,128)S(1)}, f32[2,16,128]{2,1,0:T(8,128)S(1)}, u32[]{:S(2)}, u32[]{:S(2)}) collective-permute-start(f32[2,16,128]{2,1,0:T(8,128)S(1)} %slice.13), channel_id=1, source_target_pairs={{0,64},{1,65},{2,66},{3,67},{4,68},{5,69},{6,70},{7,71},{8,72},{9,... | collective-permute-start | bytes 49160 | tf_op jit(solution)/shard_map/ppermute | solution.py:292
  24.4 0.1 pad_add_fusion.ids_ref
  24.5 8.2 %collective-permute-start = (f32[2,64,128]{2,1,0:T(8,128)S(1)}, f32[2,64,128]{2,1,0:T(8,128)S(1)}, u32[]{:S(2)}, u32[]{:S(2)}) collective-permute-start(f32[2,64,128]{2,1,0:T(8,128)S(1)} %slice.12), channel_id=1, source_target_pairs={{0,16},{1,17},{2,18},{3,19},{4,20},{5,21},{6,22},{7,23},{8,24},{9,... | collective-permute-start | bytes 196616 | tf_op jit(solution)/shard_map/ppermute | solution.py:275
  32.7 0.0 collective-permute-done.2
  32.7 1.5 %collective-permute-done.1 = f32[2,16,128]{2,1,0:T(8,128)S(1)} collective-permute-done((f32[2,16,128]{2,1,0:T(8,128)S(1)}, f32[2,16,128]{2,1,0:T(8,128)S(1)}, u32[]{:S(2)}, u32[]{:S(2)}) %collective-permute-start.1) | collective-permute-done | bytes 16416 | tf_op jit(solution)/shard_map/ppermute | solution.py:292
  34.2 1.0 collective-permute-done
  35.2 1.2 %broadcast_in_dim.11 = f32[16,2,80,128]{3,2,1,0:T(8,128)} broadcast(f32[2,80,128]{2,1,0:T(8,128)S(1)} %pad_maximum_fusion), dimensions={1,2,3} | broadcast | bytes 1392640 | tf_op jit(solution)/shard_map/broadcast_in_dim | solution.py:269
  36.4 3.7 %all-to-all-start.1 = ((f32[16,2,80,128]{3,2,1,0:T(8,128)}), f32[16,2,80,128]{3,2,1,0:T(8,128)S(1)}, u32[]{:S(2)}, u32[]{:S(2)}) async-start(f32[16,2,80,128]{3,2,1,0:T(8,128)} %broadcast_in_dim.11), calls=%async_computation.1 | async-start | bytes 2621440 | tf_op jit(solution)/shard_map/all_to_all | solution.py:266
  40.1 0.0 copy-done.4
  40.1 1.3 %collective-permute-start.4 = (f32[256,2,128]{2,1,0:T(2,128)S(1)}, f32[256,2,128]{2,1,0:T(2,128)S(1)}, u32[]{:S(2)}, u32[]{:S(2)}) collective-permute-start(f32[256,2,128]{2,1,0:T(2,128)S(1)} %copy-done.4), channel_id=1, source_target_pairs={{128,64},{160,96},{129,65},{161,97},{130,66},{162,98},{131,67},{16... | collective-permute-start | bytes 786440 | tf_op jit(solution)/shard_map/ppermute | solution.py:317
  41.4 1.3 %collective-permute-start.3 = (f32[256,2,128]{2,1,0:T(2,128)S(1)}, f32[256,2,128]{2,1,0:T(2,128)S(1)}, u32[]{:S(2)}, u32[]{:S(2)}) collective-permute-start(f32[256,2,128]{2,1,0:T(2,128)S(1)} %copy-done.4), channel_id=1, source_target_pairs={{0,64},{32,96},{1,65},{33,97},{2,66},{34,98},{3,67},{35,99},{4,68}... | collective-permute-start | bytes 786440 | tf_op jit(solution)/shard_map/ppermute | solution.py:317
  42.7 1.3 %collective-permute-start.5 = (f32[256,2,128]{2,1,0:T(2,128)S(1)}, f32[256,2,128]{2,1,0:T(2,128)S(1)}, u32[]{:S(2)}, u32[]{:S(2)}) collective-permute-start(f32[256,2,128]{2,1,0:T(2,128)S(1)} %copy-done.4), channel_id=1, source_target_pairs={{192,64},{224,96},{193,65},{225,97},{194,66},{226,98},{195,67},{22... | collective-permute-start | bytes 786440 | tf_op jit(solution)/shard_map/ppermute | solution.py:317
  44.0 5.4 %split.1 = (bf16[2,4,256,1024]{3,2,1,0:T(8,128)(2,1)S(1)}, bf16[2,4,256,1024]{3,2,1,0:T(8,128)(2,1)S(1)}, s32[3]{0:T(128)S(1)}) custom-call(s32[3]{0:T(128)S(1)} %pad_add_fusion.ids_ref, f32[1024,16,128]{2,1,0:T(8,128)} %obs_ref.3), custom_call_target="tpu_custom_call" | custom-call | bytes 21600000 | tf_op jit(solution)/shard_map/split/pallas_call | solution.py:222
  49.5 0.0 copy-start
  49.5 1.9 %copy-done = bf16[2,4,256,1024]{3,2,1,0:T(8,128)(2,1)} copy-done((bf16[2,4,256,1024]{3,2,1,0:T(8,128)(2,1)}, bf16[2,4,256,1024]{3,2,1,0:T(8,128)(2,1)S(1)}, u32[]{:S(2)}) %copy-start) | copy-done | bytes 4194328
  51.4 0.0 copy-start.2
  51.4 2.0 %copy-done.2 = bf16[2,4,256,1024]{3,2,1,0:T(8,128)(2,1)} copy-done((bf16[2,4,256,1024]{3,2,1,0:T(8,128)(2,1)}, bf16[2,4,256,1024]{3,2,1,0:T(8,128)(2,1)S(1)}, u32[]{:S(2)}) %copy-start.2) | copy-done | bytes 4194328
  53.5 0.0 collective-permute-done.4.refs_2_
  53.5 0.0 collective-permute-done.3.refs_0_
  53.5 0.0 collective-permute-done.5.refs_3_
  53.5 4.4 %all-to-all-done.1.refs_1_ = f32[16,2,80,128]{3,2,1,0:T(8,128)S(1)} async-done(((f32[16,2,80,128]{3,2,1,0:T(8,128)}), f32[16,2,80,128]{3,2,1,0:T(8,128)S(1)}, u32[]{:S(2)}, u32[]{:S(2)}) %all-to-all-start.1) | async-done | bytes 1310752 | tf_op jit(solution)/shard_map/all_to_all | solution.py:266
  57.9 2.0 %gram.1 = (f32[192,128]{1,0:T(8,128)S(1)}, f32[192,128]{1,0:T(8,128)S(1)}, f32[256,256]{1,0:T(8,128)S(1)}) custom-call(s32[3]{0:T(128)S(1)} %get-tuple-element.37.refs_0_.ids_ref, f32[16,2,80,128]{3,2,1,0:T(8,128)S(1)} %all-to-all-done.1.refs_1_), custom_call_target="tpu_custom_call" | custom-call | bytes 5400000 | tf_op jit(solution)/shard_map/gram/pallas_call | solution.py:222
  59.9 0.1 collective-permute-start.6
  60.0 0.7 panel.1
  60.7 0.6 collective-permute-done.6
  61.3 0.0 copy-start.1
  61.3 2.2 %copy-done.1 = bf16[2,4,256,1024]{3,2,1,0:T(8,128)(2,1)S(1)} copy-done((bf16[2,4,256,1024]{3,2,1,0:T(8,128)(2,1)S(1)}, bf16[2,4,256,1024]{3,2,1,0:T(8,128)(2,1)}, u32[]{:S(2)}) %copy-start.1) | copy-done | bytes 4194328
  63.5 0.0 copy-start.3
  63.5 2.2 %copy-done.3 = bf16[2,4,256,1024]{3,2,1,0:T(8,128)(2,1)S(1)} copy-done((bf16[2,4,256,1024]{3,2,1,0:T(8,128)(2,1)S(1)}, bf16[2,4,256,1024]{3,2,1,0:T(8,128)(2,1)}, u32[]{:S(2)}) %copy-start.3) | copy-done | bytes 4194328
  65.7 3.9 %product.1 = (f32[4,256,256]{2,1,0:T(8,128)S(1)}, f32[4,256,256]{2,1,0:T(8,128)S(1)}) custom-call(s32[3]{0:T(128)S(1)} %get-tuple-element.37.refs_0_.ids_ref, bf16[1024,256]{1,0:T(8,128)(2,1)S(1)} %get-tuple-element.38.phi_ref, bf16[1024,256]{1,0:T(8,128)(2,1)S(1)} %get-tuple-element.39.plo_ref, bf16[2,4,256,1024]{3,2,1,0:T(8,128)(2,1)S(1)} %copy-done.1, ...), custom_call_target="tpu_custom_call" | custom-call | bytes 25200000 | tf_op jit(solution)/shard_map/product/pallas_call | solution.py:222
  69.6 0.2 collective-permute-start.11
  69.9 2.3 %collective-permute-start.12 = (f32[256,256]{1,0:T(8,128)S(1)}, f32[256,256]{1,0:T(8,128)S(1)}, u32[]{:S(2)}, u32[]{:S(2)}) collective-permute-start(f32[256,256]{1,0:T(8,128)S(1)} %get-tuple-element.44.own_ref), channel_id=1, source_target_pairs={{64,96},{65,97},{66,98},{67,99},{68,100},{69,101},{70,102},{71,103... | collective-permute-start | bytes 786440 | tf_op jit(solution)/shard_map/ppermute | solution.py:346
  72.1 0.1 collective-permute-start.9
  72.2 1.7 %collective-permute-start.8 = (f32[192,128]{1,0:T(8,128)S(1)}, f32[192,128]{1,0:T(8,128)S(1)}, u32[]{:S(2)}, u32[]{:S(2)}) collective-permute-start(f32[192,128]{1,0:T(8,128)S(1)} %add.21), channel_id=1, source_target_pairs={{0,128},{32,160},{64,192},{96,224},{128,0},{160,32},{192,64},{224,... | collective-permute-start | bytes 294920 | tf_op jit(solution)/shard_map/ppermute | solution.py:272
  73.9 1.8 %collective-permute-start.7 = (f32[192,128]{1,0:T(8,128)S(1)}, f32[192,128]{1,0:T(8,128)S(1)}, u32[]{:S(2)}, u32[]{:S(2)}) collective-permute-start(f32[192,128]{1,0:T(8,128)S(1)} %add.21), channel_id=1, source_target_pairs={{0,64},{32,96},{64,0},{96,32},{128,192},{160,224},{192,128},{224,1... | collective-permute-start | bytes 294920 | tf_op jit(solution)/shard_map/ppermute | solution.py:272
  75.7 0.0 collective-permute-done.12.got_ref
  75.7 1.5 %prior.1.prior_ref = f32[4,256,256]{2,1,0:T(8,128)S(1)} custom-call(f32[256,256]{1,0:T(8,128)S(1)} %get-tuple-element.44.own_ref, f32[256,256]{1,0:T(8,128)S(1)} %collective-permute-done.12.got_ref, f32[256,2,128]{2,1,0:T(2,128)S(1)} %collective-permute-done.3.refs_0_, f32[256,2,128]{2,1,0:T(2,128)S(1)} %copy-done.4, ...), custom_call_target="tpu_custom_call" | custom-call | bytes 7200000 | tf_op jit(solution)/shard_map/prior/pallas_call | solution.py:222
  77.2 0.0 collective-permute-done.11.got_ref
  77.2 0.7 combine.1
  77.9 0.3 collective-permute-start.13
  78.2 1.3 %collective-permute-start.14 = (f32[256,256]{1,0:T(8,128)S(1)}, f32[256,256]{1,0:T(8,128)S(1)}, u32[]{:S(2)}, u32[]{:S(2)}) collective-permute-start(f32[256,256]{1,0:T(8,128)S(1)} %get-tuple-element.51), channel_id=1, source_target_pairs={{0,128},{32,160},{64,192},{96,224},{128,0},{160,32},{192,64},{224,... | collective-permute-start | bytes 786440 | tf_op jit(solution)/shard_map/ppermute | solution.py:272
  79.6 1.7 %collective-permute-done.9 = f32[192,128]{1,0:T(8,128)S(1)} collective-permute-done((f32[192,128]{1,0:T(8,128)S(1)}, f32[192,128]{1,0:T(8,128)S(1)}, u32[]{:S(2)}, u32[]{:S(2)}) %collective-permute-start.9) | collective-permute-done | bytes 98336 | tf_op jit(solution)/shard_map/ppermute | solution.py:272
  81.3 0.7 collective-permute-start.15
  82.0 0.0 collective-permute-done.8
  82.0 0.0 collective-permute-done.7
  82.0 0.1 collective-permute-start.10
  82.1 1.3 %collective-permute-done.10.other_ref = f32[192,128]{1,0:T(8,128)S(1)} collective-permute-done((f32[192,128]{1,0:T(8,128)S(1)}, f32[192,128]{1,0:T(8,128)S(1)}, u32[]{:S(2)}, u32[]{:S(2)}) %collective-permute-start.10) | collective-permute-done | bytes 98336 | tf_op jit(solution)/shard_map/ppermute | solution.py:272
  83.4 13.2 %factor.1.refs_1_ = f32[256,256]{1,0:T(8,128)S(1)} custom-call(s32[3]{0:T(128)S(1)} %get-tuple-element.37.refs_0_.ids_ref, f32[192,128]{1,0:T(8,128)S(1)} %add_add_fusion.kept_ref, f32[192,128]{1,0:T(8,128)S(1)} %collective-permute-done.10.other_ref), custom_call_target="tpu_custom_call" | custom-call | bytes 46800000 | tf_op jit(solution)/shard_map/factor/pallas_call | solution.py:222
  96.7 0.0 collective-permute-done.13.refs_3_
  96.7 1.9 %collective-permute-done.14.refs_4_ = f32[256,256]{1,0:T(8,128)S(1)} collective-permute-done((f32[256,256]{1,0:T(8,128)S(1)}, f32[256,256]{1,0:T(8,128)S(1)}, u32[]{:S(2)}, u32[]{:S(2)}) %collective-permute-start.14) | collective-permute-done | bytes 262176 | tf_op jit(solution)/shard_map/ppermute | solution.py:272
  98.5 6.6 %collective-permute-done.15.refs_5_ = f32[256,256]{1,0:T(8,128)S(1)} collective-permute-done((f32[256,256]{1,0:T(8,128)S(1)}, f32[256,256]{1,0:T(8,128)S(1)}, u32[]{:S(2)}, u32[]{:S(2)}) %collective-permute-start.15) | collective-permute-done | bytes 262176 | tf_op jit(solution)/shard_map/ppermute | solution.py:272
  105.1 1.8 %finish.1 = f32[256,2,128]{2,1,0:T(2,128)} custom-call(s32[3]{0:T(128)S(1)} %get-tuple-element.37.refs_0_.ids_ref, f32[256,256]{1,0:T(8,128)S(1)} %factor.1.refs_1_, f32[256,256]{1,0:T(8,128)S(1)} %get-tuple-element.49.refs_2_, f32[256,256]{1,0:T(8,128)S(1)} %collective-permute-done.13.refs_3_, f32[256,256]{1,0:T(8,128)S(1)} %collective-permute-done.14.refs_4_, ...), custom_call_target="tpu_custom_call" | custom-call | bytes 7200000 | tf_op jit(solution)/shard_map/finish/pallas_call | solution.py:222
  (7 shorter events, 0.1 us)
Async XLA Ops:
  2.3 37.8 %copy-start.4 = (f32[256,2,128]{2,1,0:T(2,128)S(1)}, f32[256,2,128]{2,1,0:T(2,128)}, u32[]{:S(2)}) copy-start(f32[256,2,128]{2,1,0:T(2,128)} %refs_1_) | copy-start | bytes 786436
  2.3 20.1 %all-to-all-start = ((f32[16,80,128]{2,1,0:T(8,128)}), f32[16,80,128]{2,1,0:T(8,128)S(1)}, u32[]{:S(2)}, u32[]{:S(2)}) async-start(f32[16,80,128]{2,1,0:T(8,128)} %pieces.1), calls=%async_computation | async-start | bytes 1310720 | tf_op jit(solution)/shard_map/all_to_all | solution.py:266
  22.4 10.2 %collective-permute-start.2 = (f32[2,16,128]{2,1,0:T(8,128)S(1)}, f32[2,16,128]{2,1,0:T(8,128)S(1)}, u32[]{:S(2)}, u32[]{:S(2)}) collective-permute-start(f32[2,16,128]{2,1,0:T(8,128)S(1)} %slice.13), channel_id=1, source_target_pairs={{0,80},{1,81},{2,82},{3,83},{4,84},{5,85},{6,86},{7,87},{8,88},{9,... | collective-permute-start | bytes 49160 | tf_op jit(solution)/shard_map/ppermute | solution.py:292
  23.1 11.1 %collective-permute-start.1 = (f32[2,16,128]{2,1,0:T(8,128)S(1)}, f32[2,16,128]{2,1,0:T(8,128)S(1)}, u32[]{:S(2)}, u32[]{:S(2)}) collective-permute-start(f32[2,16,128]{2,1,0:T(8,128)S(1)} %slice.13), channel_id=1, source_target_pairs={{0,64},{1,65},{2,66},{3,67},{4,68},{5,69},{6,70},{7,71},{8,72},{9,... | collective-permute-start | bytes 49160 | tf_op jit(solution)/shard_map/ppermute | solution.py:292
  24.5 10.7 %collective-permute-start = (f32[2,64,128]{2,1,0:T(8,128)S(1)}, f32[2,64,128]{2,1,0:T(8,128)S(1)}, u32[]{:S(2)}, u32[]{:S(2)}) collective-permute-start(f32[2,64,128]{2,1,0:T(8,128)S(1)} %slice.12), channel_id=1, source_target_pairs={{0,16},{1,17},{2,18},{3,19},{4,20},{5,21},{6,22},{7,23},{8,24},{9,... | collective-permute-start | bytes 196616 | tf_op jit(solution)/shard_map/ppermute | solution.py:275
  36.4 21.5 %all-to-all-start.1 = ((f32[16,2,80,128]{3,2,1,0:T(8,128)}), f32[16,2,80,128]{3,2,1,0:T(8,128)S(1)}, u32[]{:S(2)}, u32[]{:S(2)}) async-start(f32[16,2,80,128]{3,2,1,0:T(8,128)} %broadcast_in_dim.11), calls=%async_computation.1 | async-start | bytes 2621440 | tf_op jit(solution)/shard_map/all_to_all | solution.py:266
  40.1 13.3 %collective-permute-start.4 = (f32[256,2,128]{2,1,0:T(2,128)S(1)}, f32[256,2,128]{2,1,0:T(2,128)S(1)}, u32[]{:S(2)}, u32[]{:S(2)}) collective-permute-start(f32[256,2,128]{2,1,0:T(2,128)S(1)} %copy-done.4), channel_id=1, source_target_pairs={{128,64},{160,96},{129,65},{161,97},{130,66},{162,98},{131,67},{16... | collective-permute-start | bytes 786440 | tf_op jit(solution)/shard_map/ppermute | solution.py:317
  41.4 12.0 %collective-permute-start.3 = (f32[256,2,128]{2,1,0:T(2,128)S(1)}, f32[256,2,128]{2,1,0:T(2,128)S(1)}, u32[]{:S(2)}, u32[]{:S(2)}) collective-permute-start(f32[256,2,128]{2,1,0:T(2,128)S(1)} %copy-done.4), channel_id=1, source_target_pairs={{0,64},{32,96},{1,65},{33,97},{2,66},{34,98},{3,67},{35,99},{4,68}... | collective-permute-start | bytes 786440 | tf_op jit(solution)/shard_map/ppermute | solution.py:317
  42.7 10.7 %collective-permute-start.5 = (f32[256,2,128]{2,1,0:T(2,128)S(1)}, f32[256,2,128]{2,1,0:T(2,128)S(1)}, u32[]{:S(2)}, u32[]{:S(2)}) collective-permute-start(f32[256,2,128]{2,1,0:T(2,128)S(1)} %copy-done.4), channel_id=1, source_target_pairs={{192,64},{224,96},{193,65},{225,97},{194,66},{226,98},{195,67},{22... | collective-permute-start | bytes 786440 | tf_op jit(solution)/shard_map/ppermute | solution.py:317
  49.5 2.0 %copy-start = (bf16[2,4,256,1024]{3,2,1,0:T(8,128)(2,1)}, bf16[2,4,256,1024]{3,2,1,0:T(8,128)(2,1)S(1)}, u32[]{:S(2)}) copy-start(bf16[2,4,256,1024]{3,2,1,0:T(8,128)(2,1)S(1)} %get-tuple-element.40.ahi_ref) | copy-start | bytes 12582916
  51.4 2.0 %copy-start.2 = (bf16[2,4,256,1024]{3,2,1,0:T(8,128)(2,1)}, bf16[2,4,256,1024]{3,2,1,0:T(8,128)(2,1)S(1)}, u32[]{:S(2)}) copy-start(bf16[2,4,256,1024]{3,2,1,0:T(8,128)(2,1)S(1)} %get-tuple-element.41.alo_ref) | copy-start | bytes 12582916
  59.9 1.4 %collective-permute-start.6 = (f32[192,128]{1,0:T(8,128)S(1)}, f32[192,128]{1,0:T(8,128)S(1)}, u32[]{:S(2)}, u32[]{:S(2)}) collective-permute-start(f32[192,128]{1,0:T(8,128)S(1)} %get-tuple-element.35), channel_id=1, source_target_pairs={{0,32},{32,0},{64,96},{96,64},{128,160},{160,128},{192,224},{224,1... | collective-permute-start | bytes 294920 | tf_op jit(solution)/shard_map/ppermute | solution.py:272
  61.3 2.2 %copy-start.1 = (bf16[2,4,256,1024]{3,2,1,0:T(8,128)(2,1)S(1)}, bf16[2,4,256,1024]{3,2,1,0:T(8,128)(2,1)}, u32[]{:S(2)}) copy-start(bf16[2,4,256,1024]{3,2,1,0:T(8,128)(2,1)} %copy-done) | copy-start | bytes 12582916
  63.5 2.2 %copy-start.3 = (bf16[2,4,256,1024]{3,2,1,0:T(8,128)(2,1)S(1)}, bf16[2,4,256,1024]{3,2,1,0:T(8,128)(2,1)}, u32[]{:S(2)}) copy-start(bf16[2,4,256,1024]{3,2,1,0:T(8,128)(2,1)} %copy-done.2) | copy-start | bytes 12582916
  69.6 7.6 %collective-permute-start.11 = (f32[4,256,256]{2,1,0:T(8,128)S(1)}, f32[4,256,256]{2,1,0:T(8,128)S(1)}, u32[]{:S(2)}, u32[]{:S(2)}) collective-permute-start(f32[4,256,256]{2,1,0:T(8,128)S(1)} %get-tuple-element.43), channel_id=1, source_target_pairs={{0,32},{32,0},{64,96},{96,64},{128,160},{160,128},{192,224},{224,1... | collective-permute-start | bytes 3145736 | tf_op jit(solution)/shard_map/ppermute | solution.py:272
  69.9 5.9 %collective-permute-start.12 = (f32[256,256]{1,0:T(8,128)S(1)}, f32[256,256]{1,0:T(8,128)S(1)}, u32[]{:S(2)}, u32[]{:S(2)}) collective-permute-start(f32[256,256]{1,0:T(8,128)S(1)} %get-tuple-element.44.own_ref), channel_id=1, source_target_pairs={{64,96},{65,97},{66,98},{67,99},{68,100},{69,101},{70,102},{71,103... | collective-permute-start | bytes 786440 | tf_op jit(solution)/shard_map/ppermute | solution.py:346
  72.1 9.2 %collective-permute-start.9 = (f32[192,128]{1,0:T(8,128)S(1)}, f32[192,128]{1,0:T(8,128)S(1)}, u32[]{:S(2)}, u32[]{:S(2)}) collective-permute-start(f32[192,128]{1,0:T(8,128)S(1)} %add.21), channel_id=1, source_target_pairs={{0,192},{32,224},{64,128},{96,160},{128,64},{160,96},{192,0},{224,... | collective-permute-start | bytes 294920 | tf_op jit(solution)/shard_map/ppermute | solution.py:272
  72.2 9.8 %collective-permute-start.8 = (f32[192,128]{1,0:T(8,128)S(1)}, f32[192,128]{1,0:T(8,128)S(1)}, u32[]{:S(2)}, u32[]{:S(2)}) collective-permute-start(f32[192,128]{1,0:T(8,128)S(1)} %add.21), channel_id=1, source_target_pairs={{0,128},{32,160},{64,192},{96,224},{128,0},{160,32},{192,64},{224,... | collective-permute-start | bytes 294920 | tf_op jit(solution)/shard_map/ppermute | solution.py:272
  73.9 8.1 %collective-permute-start.7 = (f32[192,128]{1,0:T(8,128)S(1)}, f32[192,128]{1,0:T(8,128)S(1)}, u32[]{:S(2)}, u32[]{:S(2)}) collective-permute-start(f32[192,128]{1,0:T(8,128)S(1)} %add.21), channel_id=1, source_target_pairs={{0,64},{32,96},{64,0},{96,32},{128,192},{160,224},{192,128},{224,1... | collective-permute-start | bytes 294920 | tf_op jit(solution)/shard_map/ppermute | solution.py:272
  77.9 18.7 %collective-permute-start.13 = (f32[256,256]{1,0:T(8,128)S(1)}, f32[256,256]{1,0:T(8,128)S(1)}, u32[]{:S(2)}, u32[]{:S(2)}) collective-permute-start(f32[256,256]{1,0:T(8,128)S(1)} %get-tuple-element.50), channel_id=1, source_target_pairs={{0,64},{32,96},{64,0},{96,32},{128,192},{160,224},{192,128},{224,1... | collective-permute-start | bytes 786440 | tf_op jit(solution)/shard_map/ppermute | solution.py:272
  78.2 20.3 %collective-permute-start.14 = (f32[256,256]{1,0:T(8,128)S(1)}, f32[256,256]{1,0:T(8,128)S(1)}, u32[]{:S(2)}, u32[]{:S(2)}) collective-permute-start(f32[256,256]{1,0:T(8,128)S(1)} %get-tuple-element.51), channel_id=1, source_target_pairs={{0,128},{32,160},{64,192},{96,224},{128,0},{160,32},{192,64},{224,... | collective-permute-start | bytes 786440 | tf_op jit(solution)/shard_map/ppermute | solution.py:272
  81.3 23.8 %collective-permute-start.15 = (f32[256,256]{1,0:T(8,128)S(1)}, f32[256,256]{1,0:T(8,128)S(1)}, u32[]{:S(2)}, u32[]{:S(2)}) collective-permute-start(f32[256,256]{1,0:T(8,128)S(1)} %get-tuple-element.52), channel_id=1, source_target_pairs={{0,192},{32,224},{64,128},{96,160},{128,64},{160,96},{192,0},{224,... | collective-permute-start | bytes 786440 | tf_op jit(solution)/shard_map/ppermute | solution.py:272
  82.0 1.4 %collective-permute-start.10 = (f32[192,128]{1,0:T(8,128)S(1)}, f32[192,128]{1,0:T(8,128)S(1)}, u32[]{:S(2)}, u32[]{:S(2)}) collective-permute-start(f32[192,128]{1,0:T(8,128)S(1)} %add_add_fusion.kept_ref), channel_id=1, source_target_pairs={{0,32},{32,0},{64,96},{96,64},{128,160},{160,128},{192,224},{224,1... | collective-permute-start | bytes 294920 | tf_op jit(solution)/shard_map/ppermute | solution.py:272

commit v3 on v2

--- a/solution.py
+++ b/solution.py
@@ -104,23 +104,32 @@
     w_ref[h:, :h] = -dot(w11, x)
 
 
-def split_kernel(ids_ref, obs_ref, hi_ref, lo_ref, next_ref, buf, sems):
+def split_kernel(ids_ref, obs_ref, send_hi_ref, send_lo_ref, keep_hi_ref, keep_lo_ref, next_ref, buf, sems):
     rows, cycles, width = obs_ref.shape
-    own = cycles // (2 * hi_ref.shape[1])
+    own = cycles // (2 * send_hi_ref.shape[0])
     core = ids_ref[1]
     copies = [pltpu.make_async_copy(obs_ref.at[:, c, :], buf.at[c], sems.at[c]) for c in range(cycles)]
     for copy in copies:
         copy.start()
     for i in range(3):
         next_ref[i] = ids_ref[i]
-    for c, copy in enumerate(copies):
-        copy.wait()
+
+    def place(c, hi_ref, lo_ref):
         place, at = divmod(c, own)
-        z, side = divmod(place, 2)
         hi, lo = split2(buf[c].T)
-        kept = jnp.where(core == side, 1, 0)
-        hi_ref[kept, z, at * width : (at + 1) * width, :] = hi
-        lo_ref[kept, z, at * width : (at + 1) * width, :] = lo
+        hi_ref[place // 2, at * width : (at + 1) * width, :] = hi
+        lo_ref[place // 2, at * width : (at + 1) * width, :] = lo
+
+    for c in range(0, cycles, 2 * own):
+        for copy in copies[c : c + 2 * own]:
+            copy.wait()
+        for side in range(2):
+
+            @pl.when(core == side)
+            def _():
+                for e in range(own):
+                    place(c + side * own + e, keep_hi_ref, keep_lo_ref)
+                    place(c + (1 - side) * own + e, send_hi_ref, send_lo_ref)
 
 
 def prior_kernel(own_ref, got_ref, *refs):
@@ -172,14 +181,13 @@
     hi_ref[...], lo_ref[...] = split2(assembled(z_ref, n)[0])
 
 
-def product_kernel(ids_ref, phi_ref, plo_ref, ahi_ref, alo_ref, send_ref, keep_ref):
-    for side, out_ref in enumerate((send_ref, keep_ref)):
-        for z in range(out_ref.shape[0]):
-            out_ref[z] = (
-                jnp.dot(ahi_ref[side, z], phi_ref[...], preferred_element_type=F32)
-                + jnp.dot(ahi_ref[side, z], plo_ref[...], preferred_element_type=F32)
-                + jnp.dot(alo_ref[side, z], phi_ref[...], preferred_element_type=F32)
-            )
+def product_kernel(ids_ref, phi_ref, plo_ref, ahi_ref, alo_ref, out_ref):
+    for z in range(out_ref.shape[0]):
+        out_ref[z] = (
+            jnp.dot(ahi_ref[z], phi_ref[...], preferred_element_type=F32)
+            + jnp.dot(ahi_ref[z], plo_ref[...], preferred_element_type=F32)
+            + jnp.dot(alo_ref[z], phi_ref[...], preferred_element_type=F32)
+        )
 
 
 def combine_kernel(ids_ref, kept_ref, got_ref, prior_ref, *out_refs):
@@ -300,15 +308,15 @@
     prior = jnp.where(ids[0] == holder, moved[0] + moved[1], 0.0)
     ids, full = lax.optimization_barrier((ids, jnp.concatenate([rows, prior], axis=1)))
     gathered = share(full)
-    ahi, alo, ids = call(
+    *turned, ids = call(
         split_kernel,
         "split",
         6,
-        [held((2, places, own * width, obs), BF16)] * 2 + [struct((3,), jnp.int32)],
+        [held((places, own * width, obs), BF16)] * 4 + [struct((3,), jnp.int32)],
         inhbm(observations),
         ids=ids,
         specs=[anywhere()],
-        outs=[vmem(), vmem(), smem()],
+        outs=[vmem()] * 4 + [smem()],
         scratch=[pltpu.VMEM((cycles, obs, width), F32), pltpu.SemaphoreType.DMA((cycles,))],
     )
     columns = [
@@ -340,7 +348,7 @@
     prior_sums = call(
         prior_kernel,
         "prior",
-        2,
+        0.1,
         struct((places, own * width, wide)),
         prior_panel,
         lax.ppermute(prior_panel, "row", [(holder, holder + 1)]),
@@ -349,23 +357,26 @@
 
     gram = gram_keep + gram_got
     gram_far = [swap(gram, 2 * k) for k in range(1, places)]
-    sums_send, sums_keep = call(
-        product_kernel,
-        "product",
-        7,
-        [struct((places, own * width, wide))] * 2,
-        *panel,
-        pltpu.with_memory_space_constraint(ahi, pltpu.VMEM),
-        pltpu.with_memory_space_constraint(alo, pltpu.VMEM),
-        ids=gated(ids, gram),
-    )
+    def product(parts, after, name):
+        return call(
+            product_kernel,
+            name,
+            0.1,
+            struct((places, own * width, wide)),
+            *panel,
+            *[pltpu.with_memory_space_constraint(x, pltpu.VMEM) for x in parts],
+            ids=gated(ids, after),
+        )
+
+    sums_send = product(turned[:2], gram, "product_send")
     sums_got = swap(sums_send, 1)
+    sums_keep = product(turned[2:], sums_send, "product_keep")
     gram = (gram + gram_far[0]) + (gram_far[1] + gram_far[2])
     gram_other = swap(gram, 1)
     to = call(
         combine_kernel,
         "combine",
-        0.6,
+        0.1,
         [struct((own * width, wide))] * places,
         sums_keep,
         sums_got,

time: 107 us -> 104 us (0.972)
  waiting for transfers between devices: 32 us -> 26.1 us
  Pallas kernels: 31.5 us -> 33 us
  starting transfers between devices: 33.5 us -> 34.6 us
    ppermute x9, waiting for transfers between devices: 12.1 us -> 8.56 us  [swap(): return lax.ppermute(x, 'row', [(r, r ^ k) for r in range(n_row)])]
    all_to_all x2, waiting for transfers between devices: 17.4 us -> 15.1 us  [exchange(): return lax.all_to_all(x, 'col', 0, 0, tiled=True, axis_index_groups=planes)]
    pallas_call x9 -> x10, Pallas kernels: 31.5 us -> 33 us  [call(): pl.pallas_call(kernel, out_shape=out_shape, in_specs=[smem()] * len(first...]
    ppermute x9, starting transfers between devices: 6.32 us -> 7.58 us  [swap(): return lax.ppermute(x, 'row', [(r, r ^ k) for r in range(n_row)])]
    unnamed x10 -> x24, local copies, waits for them, and re-layouts: 8.35 us -> 7.81 us
  transfers between devices with their start and end apart: 18 -> 18, of which waited for: 9 -> 8; matrix products, arithmetic and copies ran while one was open for 0% -> 0% of each run, Pallas kernels for 20% -> 24%
where the time goes in v3:
time: 104 us; the launch traced here: 103 us
  starting transfers between devices  34.6 us (33%)
  Pallas kernels  33 us (32%)
  waiting for transfers between devices  26.1 us (25%)
  local copies, waits for them, and re-layouts  9.02 us (9%)
    pallas_call x10, Pallas kernels, call(): pl.pallas_call(kernel, out_shape=out_shape, in_specs=[smem()] * len(first...  33 us
    all_to_all x2, waiting for transfers between devices, exchange(): return lax.all_to_all(x, 'col', 0, 0, tiled=True, axis_index_groups=planes)  15.1 us
    all_to_all x2, starting transfers between devices, exchange(): return lax.all_to_all(x, 'col', 0, 0, tiled=True, axis_index_groups=planes)  10.7 us
    ppermute x9, waiting for transfers between devices, swap(): return lax.ppermute(x, 'row', [(r, r ^ k) for r in range(n_row)])  8.56 us
    ppermute x1, starting transfers between devices, across(): far = lax.ppermute(x, 'col', [(i, i + plane) for i in range(plane)])  8.19 us
    unnamed x24, local copies, waits for them, and re-layouts  7.81 us
    ppermute x9, starting transfers between devices, swap(): return lax.ppermute(x, 'row', [(r, r ^ k) for r in range(n_row)])  7.58 us
    ppermute x3, starting transfers between devices, local(): lax.ppermute(prior_rows, 'row', [(2 * z + core, holder + core) for core i...  3.88 us
  transfers between devices with their start and end apart: 18, of which 8 were waited for; matrix products, arithmetic and copies ran while one was open for 0% of the time, Pallas kernels for 24%

profile of v3, /device:TPU:32, one launch (start us, length us, event | category | flops | bytes accessed | tf_op | source)
XLA Modules:
  0.0 103.2 jit_solution(15939840722374871425)
XLA Ops:
  0.0 2.3 %pieces.1 = f32[16,80,128]{2,1,0:T(8,128)} custom-call(f32[1024,16,128]{2,1,0:T(8,128)} %obs_ref.3, f32[256,2,128]{2,1,0:T(2,128)} %refs_1_), custom_call_target="tpu_custom_call" | custom-call | bytes 7200000 | tf_op jit(solution)/shard_map/pieces/pallas_call | solution.py:230
  2.3 7.0 %all-to-all-start = ((f32[16,80,128]{2,1,0:T(8,128)}), f32[16,80,128]{2,1,0:T(8,128)S(1)}, u32[]{:S(2)}, u32[]{:S(2)}) async-start(f32[16,80,128]{2,1,0:T(8,128)} %pieces.1), calls=%async_computation | async-start | bytes 1310720 | tf_op jit(solution)/shard_map/all_to_all | solution.py:274
  9.4 12.9 %all-to-all-done = f32[16,80,128]{2,1,0:T(8,128)S(1)} async-done(((f32[16,80,128]{2,1,0:T(8,128)}), f32[16,80,128]{2,1,0:T(8,128)S(1)}, u32[]{:S(2)}, u32[]{:S(2)}) %all-to-all-start) | async-done | bytes 655392 | tf_op jit(solution)/shard_map/all_to_all | solution.py:274
  22.3 0.7 collective-permute-start.2
  22.9 1.3 %collective-permute-start.1 = (f32[2,16,128]{2,1,0:T(8,128)S(1)}, f32[2,16,128]{2,1,0:T(8,128)S(1)}, u32[]{:S(2)}, u32[]{:S(2)}) collective-permute-start(f32[2,16,128]{2,1,0:T(8,128)S(1)} %slice.13), channel_id=1, source_target_pairs={{0,64},{1,65},{2,66},{3,67},{4,68},{5,69},{6,70},{7,71},{8,72},{9,... | collective-permute-start | bytes 49160 | tf_op jit(solution)/shard_map/ppermute | solution.py:300
  24.2 0.1 pad_add_fusion.ids_ref
  24.3 8.2 %collective-permute-start = (f32[2,64,128]{2,1,0:T(8,128)S(1)}, f32[2,64,128]{2,1,0:T(8,128)S(1)}, u32[]{:S(2)}, u32[]{:S(2)}) collective-permute-start(f32[2,64,128]{2,1,0:T(8,128)S(1)} %slice.12), channel_id=1, source_target_pairs={{0,16},{1,17},{2,18},{3,19},{4,20},{5,21},{6,22},{7,23},{8,24},{9,... | collective-permute-start | bytes 196616 | tf_op jit(solution)/shard_map/ppermute | solution.py:283
  32.5 0.0 collective-permute-done.2
  32.5 1.5 %collective-permute-done.1 = f32[2,16,128]{2,1,0:T(8,128)S(1)} collective-permute-done((f32[2,16,128]{2,1,0:T(8,128)S(1)}, f32[2,16,128]{2,1,0:T(8,128)S(1)}, u32[]{:S(2)}, u32[]{:S(2)}) %collective-permute-start.1) | collective-permute-done | bytes 16416 | tf_op jit(solution)/shard_map/ppermute | solution.py:300
  34.0 1.0 collective-permute-done
  35.0 1.2 %broadcast_in_dim.11 = f32[16,2,80,128]{3,2,1,0:T(8,128)} broadcast(f32[2,80,128]{2,1,0:T(8,128)S(1)} %pad_maximum_fusion), dimensions={1,2,3} | broadcast | bytes 1392640 | tf_op jit(solution)/shard_map/broadcast_in_dim | solution.py:277
  36.2 3.7 %all-to-all-start.1 = ((f32[16,2,80,128]{3,2,1,0:T(8,128)}), f32[16,2,80,128]{3,2,1,0:T(8,128)S(1)}, u32[]{:S(2)}, u32[]{:S(2)}) async-start(f32[16,2,80,128]{3,2,1,0:T(8,128)} %broadcast_in_dim.11), calls=%async_computation.1 | async-start | bytes 2621440 | tf_op jit(solution)/shard_map/all_to_all | solution.py:274
  40.0 1.3 %collective-permute-start.4 = (f32[256,2,128]{2,1,0:T(2,128)}, f32[256,2,128]{2,1,0:T(2,128)S(1)}, u32[]{:S(2)}, u32[]{:S(2)}) collective-permute-start(f32[256,2,128]{2,1,0:T(2,128)} %refs_1_), channel_id=1, source_target_pairs={{128,64},{160,96},{129,65},{161,97},{130,66},{162,98},{131,67},{16... | collective-permute-start | bytes 786440 | tf_op jit(solution)/shard_map/ppermute | solution.py:325
  41.3 1.3 %collective-permute-start.3 = (f32[256,2,128]{2,1,0:T(2,128)}, f32[256,2,128]{2,1,0:T(2,128)S(1)}, u32[]{:S(2)}, u32[]{:S(2)}) collective-permute-start(f32[256,2,128]{2,1,0:T(2,128)} %refs_1_), channel_id=1, source_target_pairs={{0,64},{32,96},{1,65},{33,97},{2,66},{34,98},{3,67},{35,99},{4,68}... | collective-permute-start | bytes 786440 | tf_op jit(solution)/shard_map/ppermute | solution.py:325
  42.6 1.3 %collective-permute-start.5 = (f32[256,2,128]{2,1,0:T(2,128)}, f32[256,2,128]{2,1,0:T(2,128)S(1)}, u32[]{:S(2)}, u32[]{:S(2)}) collective-permute-start(f32[256,2,128]{2,1,0:T(2,128)} %refs_1_), channel_id=1, source_target_pairs={{192,64},{224,96},{193,65},{225,97},{194,66},{226,98},{195,67},{22... | collective-permute-start | bytes 786440 | tf_op jit(solution)/shard_map/ppermute | solution.py:325
  43.9 5.5 %split.1 = (bf16[4,256,1024]{2,1,0:T(8,128)(2,1)S(1)}, bf16[4,256,1024]{2,1,0:T(8,128)(2,1)S(1)}, bf16[4,256,1024]{2,1,0:T(8,128)(2,1)S(1)}, bf16[4,256,1024]{2,1,0:T(8,128)(2,1)S(1)}, s32[3]{0:T(128)S(1)}) custom-call(s32[3]{0:T(128)S(1)} %pad_add_fusion.ids_ref, f32[1024,16,128]{2,1,0:T(8,128)} %obs_ref.3), custom_call_target="tpu_custom_call" | custom-call | bytes 21600000 | tf_op jit(solution)/shard_map/split/pallas_call | solution.py:230
  49.4 0.0 copy-start
  49.4 1.3 %copy-done = bf16[4,256,1024]{2,1,0:T(8,128)(2,1)} copy-done((bf16[4,256,1024]{2,1,0:T(8,128)(2,1)}, bf16[4,256,1024]{2,1,0:T(8,128)(2,1)S(1)}, u32[]{:S(2)}) %copy-start) | copy-done | bytes 2097176
  50.7 0.0 copy-start.2
  50.7 1.3 %copy-done.2 = bf16[4,256,1024]{2,1,0:T(8,128)(2,1)} copy-done((bf16[4,256,1024]{2,1,0:T(8,128)(2,1)}, bf16[4,256,1024]{2,1,0:T(8,128)(2,1)S(1)}, u32[]{:S(2)}) %copy-start.2) | copy-done | bytes 2097176
  52.0 0.0 copy-start.4
  52.0 1.4 %copy-done.4 = bf16[4,256,1024]{2,1,0:T(8,128)(2,1)} copy-done((bf16[4,256,1024]{2,1,0:T(8,128)(2,1)}, bf16[4,256,1024]{2,1,0:T(8,128)(2,1)S(1)}, u32[]{:S(2)}) %copy-start.4) | copy-done | bytes 2097176
  53.4 0.0 collective-permute-done.4.refs_2_
  53.4 0.7 copy-done.6
  54.2 0.0 collective-permute-done.3.refs_0_
  54.2 0.7 copy-done.8
  54.9 0.0 collective-permute-done.5.refs_3_
  54.9 0.7 copy-done.10
  55.6 2.1 %all-to-all-done.1.refs_1_ = f32[16,2,80,128]{3,2,1,0:T(8,128)S(1)} async-done(((f32[16,2,80,128]{3,2,1,0:T(8,128)}), f32[16,2,80,128]{3,2,1,0:T(8,128)S(1)}, u32[]{:S(2)}, u32[]{:S(2)}) %all-to-all-start.1) | async-done | bytes 1310752 | tf_op jit(solution)/shard_map/all_to_all | solution.py:274
  57.7 1.9 %gram.1 = (f32[192,128]{1,0:T(8,128)S(1)}, f32[192,128]{1,0:T(8,128)S(1)}, f32[256,256]{1,0:T(8,128)S(1)}) custom-call(s32[3]{0:T(128)S(1)} %get-tuple-element.43.refs_0_.ids_ref, f32[16,2,80,128]{3,2,1,0:T(8,128)S(1)} %all-to-all-done.1.refs_1_), custom_call_target="tpu_custom_call" | custom-call | bytes 5400000 | tf_op jit(solution)/shard_map/gram/pallas_call | solution.py:230
  59.6 0.1 collective-permute-start.6
  59.7 0.7 panel.1
  60.4 0.6 collective-permute-done.6
  61.0 0.0 copy-done.3
  61.1 0.0 copy-start.5
  61.1 1.6 %copy-done.5 = bf16[4,256,1024]{2,1,0:T(8,128)(2,1)S(1)} copy-done((bf16[4,256,1024]{2,1,0:T(8,128)(2,1)S(1)}, bf16[4,256,1024]{2,1,0:T(8,128)(2,1)}, u32[]{:S(2)}) %copy-start.5) | copy-done | bytes 2097176
  62.7 2.3 %product_send.1 = f32[4,256,256]{2,1,0:T(8,128)S(1)} custom-call(s32[3]{0:T(128)S(1)} %get-tuple-element.43.refs_0_.ids_ref, bf16[1024,256]{1,0:T(8,128)(2,1)S(1)} %get-tuple-element.39.phi_ref, bf16[1024,256]{1,0:T(8,128)(2,1)S(1)} %get-tuple-element.40.plo_ref, bf16[4,256,1024]{2,1,0:T(8,128)(2,1)S(1)} %copy-done.3, bf16[4,256,1024]{2,1,0:T(8,128)(2,1)S(1)} %copy-done.5), custom_call_target="tpu_custom_call" | custom-call | bytes 360000 | tf_op jit(solution)/shard_map/product_send/pallas_call | solution.py:230
  65.0 0.2 collective-permute-start.11
  65.2 2.3 %collective-permute-start.12 = (f32[256,256]{1,0:T(8,128)S(1)}, f32[256,256]{1,0:T(8,128)S(1)}, u32[]{:S(2)}, u32[]{:S(2)}) collective-permute-start(f32[256,256]{1,0:T(8,128)S(1)} %get-tuple-element.46.own_ref), channel_id=1, source_target_pairs={{64,96},{65,97},{66,98},{67,99},{68,100},{69,101},{70,102},{71,103... | collective-permute-start | bytes 786440 | tf_op jit(solution)/shard_map/ppermute | solution.py:354
  67.5 0.1 collective-permute-start.9
  67.6 1.7 %collective-permute-start.8 = (f32[192,128]{1,0:T(8,128)S(1)}, f32[192,128]{1,0:T(8,128)S(1)}, u32[]{:S(2)}, u32[]{:S(2)}) collective-permute-start(f32[192,128]{1,0:T(8,128)S(1)} %add.21), channel_id=1, source_target_pairs={{0,128},{32,160},{64,192},{96,224},{128,0},{160,32},{192,64},{224,... | collective-permute-start | bytes 294920 | tf_op jit(solution)/shard_map/ppermute | solution.py:280
  69.3 1.8 %collective-permute-start.7 = (f32[192,128]{1,0:T(8,128)S(1)}, f32[192,128]{1,0:T(8,128)S(1)}, u32[]{:S(2)}, u32[]{:S(2)}) collective-permute-start(f32[192,128]{1,0:T(8,128)S(1)} %add.21), channel_id=1, source_target_pairs={{0,64},{32,96},{64,0},{96,32},{128,192},{160,224},{192,128},{224,1... | collective-permute-start | bytes 294920 | tf_op jit(solution)/shard_map/ppermute | solution.py:280
  71.1 0.0 copy-done.1
  71.1 2.3 %product_keep.1.kept_ref = f32[4,256,256]{2,1,0:T(8,128)S(1)} custom-call(s32[3]{0:T(128)S(1)} %get-tuple-element.43.refs_0_.ids_ref, bf16[1024,256]{1,0:T(8,128)(2,1)S(1)} %get-tuple-element.39.phi_ref, bf16[1024,256]{1,0:T(8,128)(2,1)S(1)} %get-tuple-element.40.plo_ref, bf16[4,256,1024]{2,1,0:T(8,128)(2,1)S(1)} %get-tuple-element.44.ahi_ref, ...), custom_call_target="tpu_custom_call" | custom-call | bytes 360000 | tf_op jit(solution)/shard_map/product_keep/pallas_call | solution.py:230
  73.4 0.0 collective-permute-done.12.got_ref
  73.4 0.0 copy-done.7
  73.4 0.0 copy-done.9
  73.5 0.0 copy-done.11
  73.5 2.3 %prior.1.prior_ref = f32[4,256,256]{2,1,0:T(8,128)S(1)} custom-call(f32[256,256]{1,0:T(8,128)S(1)} %get-tuple-element.46.own_ref, f32[256,256]{1,0:T(8,128)S(1)} %collective-permute-done.12.got_ref, f32[256,2,128]{2,1,0:T(2,128)S(1)} %copy-done.9, f32[256,2,128]{2,1,0:T(2,128)} %refs_1_, f32[256,2,128]{2,1,0:T(2,128)S(1)} %copy-done.7, ...), custom_call_target="tpu_custom_call" | custom-call | bytes 360000 | tf_op jit(solution)/shard_map/prior/pallas_call | solution.py:230
  75.8 0.0 collective-permute-done.11.got_ref
  75.8 0.7 combine.1
  76.5 0.3 collective-permute-start.13
  76.8 1.3 %collective-permute-start.14 = (f32[256,256]{1,0:T(8,128)S(1)}, f32[256,256]{1,0:T(8,128)S(1)}, u32[]{:S(2)}, u32[]{:S(2)}) collective-permute-start(f32[256,256]{1,0:T(8,128)S(1)} %get-tuple-element.53), channel_id=1, source_target_pairs={{0,128},{32,160},{64,192},{96,224},{128,0},{160,32},{192,64},{224,... | collective-permute-start | bytes 786440 | tf_op jit(solution)/shard_map/ppermute | solution.py:280
  78.2 0.0 collective-permute-done.9
  78.2 1.9 %collective-permute-start.15 = (f32[256,256]{1,0:T(8,128)S(1)}, f32[256,256]{1,0:T(8,128)S(1)}, u32[]{:S(2)}, u32[]{:S(2)}) collective-permute-start(f32[256,256]{1,0:T(8,128)S(1)} %get-tuple-element.54), channel_id=1, source_target_pairs={{0,192},{32,224},{64,128},{96,160},{128,64},{160,96},{192,0},{224,... | collective-permute-start | bytes 786440 | tf_op jit(solution)/shard_map/ppermute | solution.py:280
  80.1 0.0 collective-permute-done.8
  80.1 0.0 collective-permute-done.7
  80.1 0.1 collective-permute-start.10
  80.2 1.3 %collective-permute-done.10.other_ref = f32[192,128]{1,0:T(8,128)S(1)} collective-permute-done((f32[192,128]{1,0:T(8,128)S(1)}, f32[192,128]{1,0:T(8,128)S(1)}, u32[]{:S(2)}, u32[]{:S(2)}) %collective-permute-start.10) | collective-permute-done | bytes 98336 | tf_op jit(solution)/shard_map/ppermute | solution.py:280
  81.5 13.2 %factor.1.refs_1_ = f32[256,256]{1,0:T(8,128)S(1)} custom-call(s32[3]{0:T(128)S(1)} %get-tuple-element.43.refs_0_.ids_ref, f32[192,128]{1,0:T(8,128)S(1)} %add_add_fusion.kept_ref, f32[192,128]{1,0:T(8,128)S(1)} %collective-permute-done.10.other_ref), custom_call_target="tpu_custom_call" | custom-call | bytes 46800000 | tf_op jit(solution)/shard_map/factor/pallas_call | solution.py:230
  94.8 0.0 collective-permute-done.13.refs_3_
  94.8 1.4 %collective-permute-done.14.refs_4_ = f32[256,256]{1,0:T(8,128)S(1)} collective-permute-done((f32[256,256]{1,0:T(8,128)S(1)}, f32[256,256]{1,0:T(8,128)S(1)}, u32[]{:S(2)}, u32[]{:S(2)}) %collective-permute-start.14) | collective-permute-done | bytes 262176 | tf_op jit(solution)/shard_map/ppermute | solution.py:280
  96.2 5.3 %collective-permute-done.15.refs_5_ = f32[256,256]{1,0:T(8,128)S(1)} collective-permute-done((f32[256,256]{1,0:T(8,128)S(1)}, f32[256,256]{1,0:T(8,128)S(1)}, u32[]{:S(2)}, u32[]{:S(2)}) %collective-permute-start.15) | collective-permute-done | bytes 262176 | tf_op jit(solution)/shard_map/ppermute | solution.py:280
  101.4 1.8 %finish.1 = f32[256,2,128]{2,1,0:T(2,128)} custom-call(s32[3]{0:T(128)S(1)} %get-tuple-element.43.refs_0_.ids_ref, f32[256,256]{1,0:T(8,128)S(1)} %factor.1.refs_1_, f32[256,256]{1,0:T(8,128)S(1)} %get-tuple-element.51.refs_2_, f32[256,256]{1,0:T(8,128)S(1)} %collective-permute-done.13.refs_3_, f32[256,256]{1,0:T(8,128)S(1)} %collective-permute-done.14.refs_4_, ...), custom_call_target="tpu_custom_call" | custom-call | bytes 7200000 | tf_op jit(solution)/shard_map/finish/pallas_call | solution.py:230
  (15 shorter events, 0.1 us)
Async XLA Ops:
  2.3 20.0 %all-to-all-start = ((f32[16,80,128]{2,1,0:T(8,128)}), f32[16,80,128]{2,1,0:T(8,128)S(1)}, u32[]{:S(2)}, u32[]{:S(2)}) async-start(f32[16,80,128]{2,1,0:T(8,128)} %pieces.1), calls=%async_computation | async-start | bytes 1310720 | tf_op jit(solution)/shard_map/all_to_all | solution.py:274
  22.3 10.2 %collective-permute-start.2 = (f32[2,16,128]{2,1,0:T(8,128)S(1)}, f32[2,16,128]{2,1,0:T(8,128)S(1)}, u32[]{:S(2)}, u32[]{:S(2)}) collective-permute-start(f32[2,16,128]{2,1,0:T(8,128)S(1)} %slice.13), channel_id=1, source_target_pairs={{0,80},{1,81},{2,82},{3,83},{4,84},{5,85},{6,86},{7,87},{8,88},{9,... | collective-permute-start | bytes 49160 | tf_op jit(solution)/shard_map/ppermute | solution.py:300
  22.9 11.1 %collective-permute-start.1 = (f32[2,16,128]{2,1,0:T(8,128)S(1)}, f32[2,16,128]{2,1,0:T(8,128)S(1)}, u32[]{:S(2)}, u32[]{:S(2)}) collective-permute-start(f32[2,16,128]{2,1,0:T(8,128)S(1)} %slice.13), channel_id=1, source_target_pairs={{0,64},{1,65},{2,66},{3,67},{4,68},{5,69},{6,70},{7,71},{8,72},{9,... | collective-permute-start | bytes 49160 | tf_op jit(solution)/shard_map/ppermute | solution.py:300
  24.3 10.7 %collective-permute-start = (f32[2,64,128]{2,1,0:T(8,128)S(1)}, f32[2,64,128]{2,1,0:T(8,128)S(1)}, u32[]{:S(2)}, u32[]{:S(2)}) collective-permute-start(f32[2,64,128]{2,1,0:T(8,128)S(1)} %slice.12), channel_id=1, source_target_pairs={{0,16},{1,17},{2,18},{3,19},{4,20},{5,21},{6,22},{7,23},{8,24},{9,... | collective-permute-start | bytes 196616 | tf_op jit(solution)/shard_map/ppermute | solution.py:283
  36.2 21.5 %all-to-all-start.1 = ((f32[16,2,80,128]{3,2,1,0:T(8,128)}), f32[16,2,80,128]{3,2,1,0:T(8,128)S(1)}, u32[]{:S(2)}, u32[]{:S(2)}) async-start(f32[16,2,80,128]{3,2,1,0:T(8,128)} %broadcast_in_dim.11), calls=%async_computation.1 | async-start | bytes 2621440 | tf_op jit(solution)/shard_map/all_to_all | solution.py:274
  40.0 13.5 %collective-permute-start.4 = (f32[256,2,128]{2,1,0:T(2,128)}, f32[256,2,128]{2,1,0:T(2,128)S(1)}, u32[]{:S(2)}, u32[]{:S(2)}) collective-permute-start(f32[256,2,128]{2,1,0:T(2,128)} %refs_1_), channel_id=1, source_target_pairs={{128,64},{160,96},{129,65},{161,97},{130,66},{162,98},{131,67},{16... | collective-permute-start | bytes 786440 | tf_op jit(solution)/shard_map/ppermute | solution.py:325
  41.3 12.9 %collective-permute-start.3 = (f32[256,2,128]{2,1,0:T(2,128)}, f32[256,2,128]{2,1,0:T(2,128)S(1)}, u32[]{:S(2)}, u32[]{:S(2)}) collective-permute-start(f32[256,2,128]{2,1,0:T(2,128)} %refs_1_), channel_id=1, source_target_pairs={{0,64},{32,96},{1,65},{33,97},{2,66},{34,98},{3,67},{35,99},{4,68}... | collective-permute-start | bytes 786440 | tf_op jit(solution)/shard_map/ppermute | solution.py:325
  42.6 12.3 %collective-permute-start.5 = (f32[256,2,128]{2,1,0:T(2,128)}, f32[256,2,128]{2,1,0:T(2,128)S(1)}, u32[]{:S(2)}, u32[]{:S(2)}) collective-permute-start(f32[256,2,128]{2,1,0:T(2,128)} %refs_1_), channel_id=1, source_target_pairs={{192,64},{224,96},{193,65},{225,97},{194,66},{226,98},{195,67},{22... | collective-permute-start | bytes 786440 | tf_op jit(solution)/shard_map/ppermute | solution.py:325
  49.4 1.3 %copy-start = (bf16[4,256,1024]{2,1,0:T(8,128)(2,1)}, bf16[4,256,1024]{2,1,0:T(8,128)(2,1)S(1)}, u32[]{:S(2)}) copy-start(bf16[4,256,1024]{2,1,0:T(8,128)(2,1)S(1)} %get-tuple-element.45.alo_ref) | copy-start | bytes 6291460
  50.7 1.3 %copy-start.2 = (bf16[4,256,1024]{2,1,0:T(8,128)(2,1)}, bf16[4,256,1024]{2,1,0:T(8,128)(2,1)S(1)}, u32[]{:S(2)}) copy-start(bf16[4,256,1024]{2,1,0:T(8,128)(2,1)S(1)} %get-tuple-element.41.ahi_ref) | copy-start | bytes 6291460
  52.0 1.4 %copy-start.4 = (bf16[4,256,1024]{2,1,0:T(8,128)(2,1)}, bf16[4,256,1024]{2,1,0:T(8,128)(2,1)S(1)}, u32[]{:S(2)}) copy-start(bf16[4,256,1024]{2,1,0:T(8,128)(2,1)S(1)} %get-tuple-element.42.alo_ref) | copy-start | bytes 6291460
  53.4 0.7 copy-start.6
  54.2 0.7 copy-start.8
  54.9 0.7 copy-start.10
  57.7 3.3 %copy-start.3 = (bf16[4,256,1024]{2,1,0:T(8,128)(2,1)S(1)}, bf16[4,256,1024]{2,1,0:T(8,128)(2,1)}, u32[]{:S(2)}) copy-start(bf16[4,256,1024]{2,1,0:T(8,128)(2,1)} %copy-done.2) | copy-start | bytes 6291460
  59.6 1.4 %collective-permute-start.6 = (f32[192,128]{1,0:T(8,128)S(1)}, f32[192,128]{1,0:T(8,128)S(1)}, u32[]{:S(2)}, u32[]{:S(2)}) collective-permute-start(f32[192,128]{1,0:T(8,128)S(1)} %get-tuple-element.36), channel_id=1, source_target_pairs={{0,32},{32,0},{64,96},{96,64},{128,160},{160,128},{192,224},{224,1... | collective-permute-start | bytes 294920 | tf_op jit(solution)/shard_map/ppermute | solution.py:280
  61.1 1.6 %copy-start.5 = (bf16[4,256,1024]{2,1,0:T(8,128)(2,1)S(1)}, bf16[4,256,1024]{2,1,0:T(8,128)(2,1)}, u32[]{:S(2)}) copy-start(bf16[4,256,1024]{2,1,0:T(8,128)(2,1)} %copy-done.4) | copy-start | bytes 6291460
  62.7 8.4 %copy-start.1 = (bf16[4,256,1024]{2,1,0:T(8,128)(2,1)S(1)}, bf16[4,256,1024]{2,1,0:T(8,128)(2,1)}, u32[]{:S(2)}) copy-start(bf16[4,256,1024]{2,1,0:T(8,128)(2,1)} %copy-done) | copy-start | bytes 6291460
  65.0 10.8 %collective-permute-start.11 = (f32[4,256,256]{2,1,0:T(8,128)S(1)}, f32[4,256,256]{2,1,0:T(8,128)S(1)}, u32[]{:S(2)}, u32[]{:S(2)}) collective-permute-start(f32[4,256,256]{2,1,0:T(8,128)S(1)} %product_send.1), channel_id=1, source_target_pairs={{0,32},{32,0},{64,96},{96,64},{128,160},{160,128},{192,224},{224,1... | collective-permute-start | bytes 3145736 | tf_op jit(solution)/shard_map/ppermute | solution.py:280
  65.2 8.2 %collective-permute-start.12 = (f32[256,256]{1,0:T(8,128)S(1)}, f32[256,256]{1,0:T(8,128)S(1)}, u32[]{:S(2)}, u32[]{:S(2)}) collective-permute-start(f32[256,256]{1,0:T(8,128)S(1)} %get-tuple-element.46.own_ref), channel_id=1, source_target_pairs={{64,96},{65,97},{66,98},{67,99},{68,100},{69,101},{70,102},{71,103... | collective-permute-start | bytes 786440 | tf_op jit(solution)/shard_map/ppermute | solution.py:354
  67.5 10.7 %collective-permute-start.9 = (f32[192,128]{1,0:T(8,128)S(1)}, f32[192,128]{1,0:T(8,128)S(1)}, u32[]{:S(2)}, u32[]{:S(2)}) collective-permute-start(f32[192,128]{1,0:T(8,128)S(1)} %add.21), channel_id=1, source_target_pairs={{0,192},{32,224},{64,128},{96,160},{128,64},{160,96},{192,0},{224,... | collective-permute-start | bytes 294920 | tf_op jit(solution)/shard_map/ppermute | solution.py:280
  67.6 12.5 %collective-permute-start.8 = (f32[192,128]{1,0:T(8,128)S(1)}, f32[192,128]{1,0:T(8,128)S(1)}, u32[]{:S(2)}, u32[]{:S(2)}) collective-permute-start(f32[192,128]{1,0:T(8,128)S(1)} %add.21), channel_id=1, source_target_pairs={{0,128},{32,160},{64,192},{96,224},{128,0},{160,32},{192,64},{224,... | collective-permute-start | bytes 294920 | tf_op jit(solution)/shard_map/ppermute | solution.py:280
  69.3 10.8 %collective-permute-start.7 = (f32[192,128]{1,0:T(8,128)S(1)}, f32[192,128]{1,0:T(8,128)S(1)}, u32[]{:S(2)}, u32[]{:S(2)}) collective-permute-start(f32[192,128]{1,0:T(8,128)S(1)} %add.21), channel_id=1, source_target_pairs={{0,64},{32,96},{64,0},{96,32},{128,192},{160,224},{192,128},{224,1... | collective-permute-start | bytes 294920 | tf_op jit(solution)/shard_map/ppermute | solution.py:280
  71.1 2.4 %copy-start.7 = (f32[256,2,128]{2,1,0:T(2,128)S(1)}, f32[256,2,128]{2,1,0:T(2,128)}, u32[]{:S(2)}) copy-start(f32[256,2,128]{2,1,0:T(2,128)} %copy-done.6) | copy-start | bytes 786436
  71.1 2.4 %copy-start.9 = (f32[256,2,128]{2,1,0:T(2,128)S(1)}, f32[256,2,128]{2,1,0:T(2,128)}, u32[]{:S(2)}) copy-start(f32[256,2,128]{2,1,0:T(2,128)} %copy-done.8) | copy-start | bytes 786436
  71.1 2.4 %copy-start.11 = (f32[256,2,128]{2,1,0:T(2,128)S(1)}, f32[256,2,128]{2,1,0:T(2,128)}, u32[]{:S(2)}) copy-start(f32[256,2,128]{2,1,0:T(2,128)} %copy-done.10) | copy-start | bytes 786436
  76.5 18.2 %collective-permute-start.13 = (f32[256,256]{1,0:T(8,128)S(1)}, f32[256,256]{1,0:T(8,128)S(1)}, u32[]{:S(2)}, u32[]{:S(2)}) collective-permute-start(f32[256,256]{1,0:T(8,128)S(1)} %get-tuple-element.52), channel_id=1, source_target_pairs={{0,64},{32,96},{64,0},{96,32},{128,192},{160,224},{192,128},{224,1... | collective-permute-start | bytes 786440 | tf_op jit(solution)/shard_map/ppermute | solution.py:280
  76.8 19.3 %collective-permute-start.14 = (f32[256,256]{1,0:T(8,128)S(1)}, f32[256,256]{1,0:T(8,128)S(1)}, u32[]{:S(2)}, u32[]{:S(2)}) collective-permute-start(f32[256,256]{1,0:T(8,128)S(1)} %get-tuple-element.53), channel_id=1, source_target_pairs={{0,128},{32,160},{64,192},{96,224},{128,0},{160,32},{192,64},{224,... | collective-permute-start | bytes 786440 | tf_op jit(solution)/shard_map/ppermute | solution.py:280
  78.2 23.3 %collective-permute-start.15 = (f32[256,256]{1,0:T(8,128)S(1)}, f32[256,256]{1,0:T(8,128)S(1)}, u32[]{:S(2)}, u32[]{:S(2)}) collective-permute-start(f32[256,256]{1,0:T(8,128)S(1)} %get-tuple-element.54), channel_id=1, source_target_pairs={{0,192},{32,224},{64,128},{96,160},{128,64},{160,96},{192,0},{224,... | collective-permute-start | bytes 786440 | tf_op jit(solution)/shard_map/ppermute | solution.py:280
  80.1 1.4 %collective-permute-start.10 = (f32[192,128]{1,0:T(8,128)S(1)}, f32[192,128]{1,0:T(8,128)S(1)}, u32[]{:S(2)}, u32[]{:S(2)}) collective-permute-start(f32[192,128]{1,0:T(8,128)S(1)} %add_add_fusion.kept_ref), channel_id=1, source_target_pairs={{0,32},{32,0},{64,96},{96,64},{128,160},{160,128},{192,224},{224,1... | collective-permute-start | bytes 294920 | tf_op jit(solution)/shard_map/ppermute | solution.py:280

commit v4 on v3

--- a/solution.py
+++ b/solution.py
@@ -295,18 +295,10 @@
         scratch=[pltpu.SemaphoreType.DMA((plane,))] * 2,
     )
     got = exchange(pieces)[:panels]
-    holder = 2
-    moved = [
-        lax.ppermute(
-            got[:, each:, :],
-            ("row", "col"),
-            [(c, holder * n_col + c + h * plane) for c in range(plane)],
-        )
-        for h in range(2)
-    ]
-    rows = across(got[:, :each, :])
-    prior = jnp.where(ids[0] == holder, moved[0] + moved[1], 0.0)
-    ids, full = lax.optimization_barrier((ids, jnp.concatenate([rows, prior], axis=1)))
+    holder = 0
+    prior_at = lax.broadcasted_iota(jnp.int32, got.shape, 1) >= each
+    full = jnp.where(prior_at & (row_pos != holder), 0.0, across(got))
+    ids, full = lax.optimization_barrier((ids, full))
     gathered = share(full)
     *turned, ids = call(
         split_kernel,
@@ -326,7 +318,7 @@
         for z in range(places)
     ]
 
-    gathered, ids, *columns = lax.optimization_barrier((gathered, ids, *columns))
+    gathered, ids, columns[1] = lax.optimization_barrier((gathered, ids, columns[1]))
     gram_keep, gram_send, prior_panel = call(
         lambda *refs: gram_kernel(each, *refs),
         "gram",
@@ -368,6 +360,7 @@
             ids=gated(ids, after),
         )
 
+    gram, columns[2], columns[3] = lax.optimization_barrier((gram, columns[2], columns[3]))
     sums_send = product(turned[:2], gram, "product_send")
     sums_got = swap(sums_send, 1)
     sums_keep = product(turned[2:], sums_send, "product_keep")

time: 104 us -> 104 us (level)
  local copies, waits for them, and re-layouts: 9.02 us -> 7.49 us
    ppermute x3, waiting for transfers between devices: 0.01 us -> 2.79 us  [local(): lax.ppermute(prior_rows, 'row', [(2 * z + core, holder + core) for core i...]
    ppermute x9, starting transfers between devices: 7.58 us -> 10.3 us  [swap(): return lax.ppermute(x, 'row', [(r, r ^ k) for r in range(n_row)])]
    all_to_all x2, waiting for transfers between devices: 15.1 us -> 13.1 us  [exchange(): return lax.all_to_all(x, 'col', 0, 0, tiled=True, axis_index_groups=planes)]
    ppermute x2 -> x0, starting transfers between devices: 1.94 us -> none  [local(): lax.ppermute(got[:, each:, :], ('row', 'col'), [(c, holder * n_col + c +...]
    ppermute x3, starting transfers between devices: 3.88 us -> 5.68 us  [local(): lax.ppermute(prior_rows, 'row', [(2 * z + core, holder + core) for core i...]
    ppermute x1, starting transfers between devices: 2.26 us -> 0.67 us  [local(): lax.ppermute(prior_panel, 'row', [(holder, holder + 1)])]
    unnamed x24 -> x16, local copies, waits for them, and re-layouts: 7.81 us -> 6.29 us
    ppermute x2 -> x0, waiting for transfers between devices: 1.5 us -> none  [local(): lax.ppermute(got[:, each:, :], ('row', 'col'), [(c, holder * n_col + c +...]
  transfers between devices with their start and end apart: 18 -> 16, of which waited for: 8 -> 8; matrix products, arithmetic and copies ran while one was open for 0% -> 0% of each run, Pallas kernels for 24% -> 26%
where the time goes in v4:
time: 104 us; the launch traced here: 103 us
  starting transfers between devices  35.6 us (34%)
  Pallas kernels  33.2 us (32%)
  waiting for transfers between devices  26.7 us (26%)
  local copies, waits for them, and re-layouts  7.49 us (7%)
    pallas_call x10, Pallas kernels, call(): pl.pallas_call(kernel, out_shape=out_shape, in_specs=[smem()] * len(first...  33.2 us
    all_to_all x2, waiting for transfers between devices, exchange(): return lax.all_to_all(x, 'col', 0, 0, tiled=True, axis_index_groups=planes)  13.1 us
    all_to_all x2, starting transfers between devices, exchange(): return lax.all_to_all(x, 'col', 0, 0, tiled=True, axis_index_groups=planes)  10.7 us
    ppermute x9, starting transfers between devices, swap(): return lax.ppermute(x, 'row', [(r, r ^ k) for r in range(n_row)])  10.3 us
    ppermute x9, waiting for transfers between devices, swap(): return lax.ppermute(x, 'row', [(r, r ^ k) for r in range(n_row)])  8.84 us
    ppermute x1, starting transfers between devices, across(): far = lax.ppermute(x, 'col', [(i, i + plane) for i in range(plane)])  8.19 us
    unnamed x16, local copies, waits for them, and re-layouts  6.29 us
    ppermute x3, starting transfers between devices, local(): lax.ppermute(prior_rows, 'row', [(2 * z + core, holder + core) for core i...  5.68 us
  transfers between devices with their start and end apart: 16, of which 8 were waited for; matrix products, arithmetic and copies ran while one was open for 0% of the time, Pallas kernels for 26%

profile of v4, /device:TPU:32, one launch (start us, length us, event | category | flops | bytes accessed | tf_op | source)
XLA Modules:
  0.0 103.4 jit_solution(9174731395298953085)
XLA Ops:
  0.0 2.3 %pieces.1 = f32[16,80,128]{2,1,0:T(8,128)} custom-call(f32[1024,16,128]{2,1,0:T(8,128)} %obs_ref.3, f32[256,2,128]{2,1,0:T(2,128)} %refs_0_.1), custom_call_target="tpu_custom_call" | custom-call | bytes 7200000 | tf_op jit(solution)/shard_map/pieces/pallas_call | solution.py:230
  2.3 7.0 %all-to-all-start = ((f32[16,80,128]{2,1,0:T(8,128)}), f32[16,80,128]{2,1,0:T(8,128)S(1)}, u32[]{:S(2)}, u32[]{:S(2)}) async-start(f32[16,80,128]{2,1,0:T(8,128)} %pieces.1), calls=%async_computation | async-start | bytes 1310720 | tf_op jit(solution)/shard_map/all_to_all | solution.py:274
  9.4 12.9 %all-to-all-done = f32[16,80,128]{2,1,0:T(8,128)S(1)} async-done(((f32[16,80,128]{2,1,0:T(8,128)}), f32[16,80,128]{2,1,0:T(8,128)S(1)}, u32[]{:S(2)}, u32[]{:S(2)}) %all-to-all-start) | async-done | bytes 655392 | tf_op jit(solution)/shard_map/all_to_all | solution.py:274
  22.3 8.2 %collective-permute-start = (f32[2,80,128]{2,1,0:T(8,128)S(1)}, f32[2,80,128]{2,1,0:T(8,128)S(1)}, u32[]{:S(2)}, u32[]{:S(2)}) collective-permute-start(f32[2,80,128]{2,1,0:T(8,128)S(1)} %slice.4), channel_id=1, source_target_pairs={{0,16},{1,17},{2,18},{3,19},{4,20},{5,21},{6,22},{7,23},{8,24},{9,... | collective-permute-start | bytes 245768 | tf_op jit(solution)/shard_map/ppermute | solution.py:283
  30.5 0.1 pad_add_fusion.ids_ref
  30.6 2.0 %collective-permute-done = f32[2,80,128]{2,1,0:T(8,128)S(1)} collective-permute-done((f32[2,80,128]{2,1,0:T(8,128)S(1)}, f32[2,80,128]{2,1,0:T(8,128)S(1)}, u32[]{:S(2)}, u32[]{:S(2)}) %collective-permute-start) | collective-permute-done | bytes 81952 | tf_op jit(solution)/shard_map/ppermute | solution.py:283
  32.5 0.1 select_select_fusion
  32.6 1.2 %broadcast_in_dim.11 = f32[16,2,80,128]{3,2,1,0:T(8,128)} broadcast(f32[2,80,128]{2,1,0:T(8,128)S(1)} %select_select_fusion), dimensions={1,2,3} | broadcast | bytes 1392640 | tf_op jit(solution)/shard_map/broadcast_in_dim | solution.py:277
  33.8 3.7 %all-to-all-start.1 = ((f32[16,2,80,128]{3,2,1,0:T(8,128)}), f32[16,2,80,128]{3,2,1,0:T(8,128)S(1)}, u32[]{:S(2)}, u32[]{:S(2)}) async-start(f32[16,2,80,128]{3,2,1,0:T(8,128)} %broadcast_in_dim.11), calls=%async_computation.1 | async-start | bytes 2621440 | tf_op jit(solution)/shard_map/all_to_all | solution.py:274
  37.5 2.9 %collective-permute-start.1 = (f32[256,2,128]{2,1,0:T(2,128)}, f32[256,2,128]{2,1,0:T(2,128)S(1)}, u32[]{:S(2)}, u32[]{:S(2)}) collective-permute-start(f32[256,2,128]{2,1,0:T(2,128)} %refs_0_.1), channel_id=1, source_target_pairs={{64,0},{96,32},{65,1},{97,33},{66,2},{98,34},{67,3},{99,35},{68,4}... | collective-permute-start | bytes 786440 | tf_op jit(solution)/shard_map/ppermute | solution.py:317
  40.4 1.4 %collective-permute-start.3 = (f32[256,2,128]{2,1,0:T(2,128)}, f32[256,2,128]{2,1,0:T(2,128)}, u32[]{:S(2)}, u32[]{:S(2)}) collective-permute-start(f32[256,2,128]{2,1,0:T(2,128)} %refs_0_.1), channel_id=1, source_target_pairs={{128,0},{160,32},{129,1},{161,33},{130,2},{162,34},{131,3},{163,35... | collective-permute-start | bytes 786440 | tf_op jit(solution)/shard_map/ppermute | solution.py:317
  41.8 1.4 %collective-permute-start.4 = (f32[256,2,128]{2,1,0:T(2,128)}, f32[256,2,128]{2,1,0:T(2,128)}, u32[]{:S(2)}, u32[]{:S(2)}) collective-permute-start(f32[256,2,128]{2,1,0:T(2,128)} %refs_0_.1), channel_id=1, source_target_pairs={{192,0},{224,32},{193,1},{225,33},{194,2},{226,34},{195,3},{227,35... | collective-permute-start | bytes 786440 | tf_op jit(solution)/shard_map/ppermute | solution.py:317
  43.2 5.5 %split.1 = (bf16[4,256,1024]{2,1,0:T(8,128)(2,1)S(1)}, bf16[4,256,1024]{2,1,0:T(8,128)(2,1)S(1)}, bf16[4,256,1024]{2,1,0:T(8,128)(2,1)S(1)}, bf16[4,256,1024]{2,1,0:T(8,128)(2,1)S(1)}, s32[3]{0:T(128)S(1)}) custom-call(s32[3]{0:T(128)S(1)} %pad_add_fusion.ids_ref, f32[1024,16,128]{2,1,0:T(8,128)} %obs_ref.3), custom_call_target="tpu_custom_call" | custom-call | bytes 21600000 | tf_op jit(solution)/shard_map/split/pallas_call | solution.py:230
  48.7 0.0 copy-start
  48.7 1.3 %copy-done = bf16[4,256,1024]{2,1,0:T(8,128)(2,1)} copy-done((bf16[4,256,1024]{2,1,0:T(8,128)(2,1)}, bf16[4,256,1024]{2,1,0:T(8,128)(2,1)S(1)}, u32[]{:S(2)}) %copy-start) | copy-done | bytes 2097176
  50.0 0.0 copy-start.2
  50.0 1.3 %copy-done.2 = bf16[4,256,1024]{2,1,0:T(8,128)(2,1)} copy-done((bf16[4,256,1024]{2,1,0:T(8,128)(2,1)}, bf16[4,256,1024]{2,1,0:T(8,128)(2,1)S(1)}, u32[]{:S(2)}) %copy-start.2) | copy-done | bytes 2097176
  51.3 0.0 copy-start.4
  51.3 1.4 %copy-done.4 = bf16[4,256,1024]{2,1,0:T(8,128)(2,1)} copy-done((bf16[4,256,1024]{2,1,0:T(8,128)(2,1)}, bf16[4,256,1024]{2,1,0:T(8,128)(2,1)S(1)}, u32[]{:S(2)}) %copy-start.4) | copy-done | bytes 2097176
  52.7 2.8 %collective-permute-done.1.refs_1_ = f32[256,2,128]{2,1,0:T(2,128)S(1)} collective-permute-done((f32[256,2,128]{2,1,0:T(2,128)}, f32[256,2,128]{2,1,0:T(2,128)S(1)}, u32[]{:S(2)}, u32[]{:S(2)}) %collective-permute-start.1) | collective-permute-done | bytes 262176 | tf_op jit(solution)/shard_map/ppermute | solution.py:317
  55.5 0.0 copy-start.6
  55.5 0.7 copy-done.6
  56.2 0.2 all-to-all-done.1.refs_1_
  56.4 0.0 copy-start.3
  56.4 1.9 %gram.1 = (f32[192,128]{1,0:T(8,128)S(1)}, f32[192,128]{1,0:T(8,128)S(1)}, f32[256,256]{1,0:T(8,128)S(1)}) custom-call(s32[3]{0:T(128)S(1)} %get-tuple-element.42.refs_0_.ids_ref, f32[16,2,80,128]{3,2,1,0:T(8,128)S(1)} %all-to-all-done.1.refs_1_), custom_call_target="tpu_custom_call" | custom-call | bytes 5400000 | tf_op jit(solution)/shard_map/gram/pallas_call | solution.py:230
  58.3 0.1 collective-permute-start.2
  58.4 0.7 panel.1
  59.1 0.6 collective-permute-done.2
  59.7 0.0 collective-permute-done.3.refs_2_
  59.7 0.0 collective-permute-done.4.refs_3_
  59.7 0.0 copy-done.3
  59.7 0.0 copy-start.5
  59.7 1.6 %copy-done.5 = bf16[4,256,1024]{2,1,0:T(8,128)(2,1)S(1)} copy-done((bf16[4,256,1024]{2,1,0:T(8,128)(2,1)S(1)}, bf16[4,256,1024]{2,1,0:T(8,128)(2,1)}, u32[]{:S(2)}) %copy-start.5) | copy-done | bytes 2097176
  61.3 0.0 copy-start.1
  61.3 2.3 %product_send.1 = f32[4,256,256]{2,1,0:T(8,128)S(1)} custom-call(s32[3]{0:T(128)S(1)} %get-tuple-element.42.refs_0_.ids_ref, bf16[1024,256]{1,0:T(8,128)(2,1)S(1)} %get-tuple-element.38.phi_ref, bf16[1024,256]{1,0:T(8,128)(2,1)S(1)} %get-tuple-element.39.plo_ref, bf16[4,256,1024]{2,1,0:T(8,128)(2,1)S(1)} %copy-done.3, bf16[4,256,1024]{2,1,0:T(8,128)(2,1)S(1)} %copy-done.5), custom_call_target="tpu_custom_call" | custom-call | bytes 360000 | tf_op jit(solution)/shard_map/product_send/pallas_call | solution.py:230
  63.7 0.2 collective-permute-start.9
  63.9 0.7 collective-permute-start.10
  64.6 1.1 %collective-permute-start.7 = (f32[192,128]{1,0:T(8,128)S(1)}, f32[192,128]{1,0:T(8,128)S(1)}, u32[]{:S(2)}, u32[]{:S(2)}) collective-permute-start(f32[192,128]{1,0:T(8,128)S(1)} %add.17), channel_id=1, source_target_pairs={{0,192},{32,224},{64,128},{96,160},{128,64},{160,96},{192,0},{224,... | collective-permute-start | bytes 294920 | tf_op jit(solution)/shard_map/ppermute | solution.py:280
  65.7 5.1 %collective-permute-start.6 = (f32[192,128]{1,0:T(8,128)S(1)}, f32[192,128]{1,0:T(8,128)S(1)}, u32[]{:S(2)}, u32[]{:S(2)}) collective-permute-start(f32[192,128]{1,0:T(8,128)S(1)} %add.17), channel_id=1, source_target_pairs={{0,128},{32,160},{64,192},{96,224},{128,0},{160,32},{192,64},{224,... | collective-permute-start | bytes 294920 | tf_op jit(solution)/shard_map/ppermute | solution.py:280
  70.8 0.0 collective-permute-start.5
  70.8 0.0 copy-done.1
  70.8 0.0 copy-start.7
  70.8 2.3 %product_keep.1.kept_ref = f32[4,256,256]{2,1,0:T(8,128)S(1)} custom-call(s32[3]{0:T(128)S(1)} %get-tuple-element.42.refs_0_.ids_ref, bf16[1024,256]{1,0:T(8,128)(2,1)S(1)} %get-tuple-element.38.phi_ref, bf16[1024,256]{1,0:T(8,128)(2,1)S(1)} %get-tuple-element.39.plo_ref, bf16[4,256,1024]{2,1,0:T(8,128)(2,1)S(1)} %get-tuple-element.43.ahi_ref, ...), custom_call_target="tpu_custom_call" | custom-call | bytes 360000 | tf_op jit(solution)/shard_map/product_keep/pallas_call | solution.py:230
  73.1 0.0 collective-permute-done.10.got_ref
  73.2 0.0 copy-done.7
  73.2 2.5 %prior.1.prior_ref = f32[4,256,256]{2,1,0:T(8,128)S(1)} custom-call(f32[256,256]{1,0:T(8,128)S(1)} %get-tuple-element.45.own_ref, f32[256,256]{1,0:T(8,128)S(1)} %collective-permute-done.10.got_ref, f32[256,2,128]{2,1,0:T(2,128)} %refs_0_.1, f32[256,2,128]{2,1,0:T(2,128)S(1)} %copy-done.7, f32[256,2,128]{2,1,0:T(2,128)} %collective-permute-done.3.refs_2_, ...), custom_call_target="tpu_custom_call" | custom-call | bytes 360000 | tf_op jit(solution)/shard_map/prior/pallas_call | solution.py:230
  75.6 0.0 collective-permute-done.9.got_ref
  75.7 0.7 combine.1
  76.4 2.1 %collective-permute-start.11 = (f32[256,256]{1,0:T(8,128)S(1)}, f32[256,256]{1,0:T(8,128)S(1)}, u32[]{:S(2)}, u32[]{:S(2)}) collective-permute-start(f32[256,256]{1,0:T(8,128)S(1)} %get-tuple-element.48), channel_id=1, source_target_pairs={{0,64},{32,96},{64,0},{96,32},{128,192},{160,224},{192,128},{224,1... | collective-permute-start | bytes 786440 | tf_op jit(solution)/shard_map/ppermute | solution.py:280
  78.5 0.0 collective-permute-start.12
  78.5 0.0 collective-permute-done.7
  78.5 1.6 %collective-permute-start.13 = (f32[256,256]{1,0:T(8,128)S(1)}, f32[256,256]{1,0:T(8,128)S(1)}, u32[]{:S(2)}, u32[]{:S(2)}) collective-permute-start(f32[256,256]{1,0:T(8,128)S(1)} %get-tuple-element.50), channel_id=1, source_target_pairs={{0,192},{32,224},{64,128},{96,160},{128,64},{160,96},{192,0},{224,... | collective-permute-start | bytes 786440 | tf_op jit(solution)/shard_map/ppermute | solution.py:280
  80.0 0.0 collective-permute-done.6
  80.0 0.0 collective-permute-done.5
  80.1 0.1 collective-permute-start.8
  80.2 1.3 %collective-permute-done.8.other_ref = f32[192,128]{1,0:T(8,128)S(1)} collective-permute-done((f32[192,128]{1,0:T(8,128)S(1)}, f32[192,128]{1,0:T(8,128)S(1)}, u32[]{:S(2)}, u32[]{:S(2)}) %collective-permute-start.8) | collective-permute-done | bytes 98336 | tf_op jit(solution)/shard_map/ppermute | solution.py:280
  81.5 13.2 %factor.1.refs_1_ = f32[256,256]{1,0:T(8,128)S(1)} custom-call(s32[3]{0:T(128)S(1)} %get-tuple-element.42.refs_0_.ids_ref, f32[192,128]{1,0:T(8,128)S(1)} %add_add_fusion.kept_ref, f32[192,128]{1,0:T(8,128)S(1)} %collective-permute-done.8.other_ref), custom_call_target="tpu_custom_call" | custom-call | bytes 46800000 | tf_op jit(solution)/shard_map/factor/pallas_call | solution.py:230
  94.7 0.0 collective-permute-done.11.refs_3_
  94.7 1.8 %collective-permute-done.12.refs_4_ = f32[256,256]{1,0:T(8,128)S(1)} collective-permute-done((f32[256,256]{1,0:T(8,128)S(1)}, f32[256,256]{1,0:T(8,128)S(1)}, u32[]{:S(2)}, u32[]{:S(2)}) %collective-permute-start.12) | collective-permute-done | bytes 262176 | tf_op jit(solution)/shard_map/ppermute | solution.py:280
  96.5 5.2 %collective-permute-done.13.refs_5_ = f32[256,256]{1,0:T(8,128)S(1)} collective-permute-done((f32[256,256]{1,0:T(8,128)S(1)}, f32[256,256]{1,0:T(8,128)S(1)}, u32[]{:S(2)}, u32[]{:S(2)}) %collective-permute-start.13) | collective-permute-done | bytes 262176 | tf_op jit(solution)/shard_map/ppermute | solution.py:280
  101.7 1.8 %finish.1 = f32[256,2,128]{2,1,0:T(2,128)} custom-call(s32[3]{0:T(128)S(1)} %get-tuple-element.42.refs_0_.ids_ref, f32[256,256]{1,0:T(8,128)S(1)} %factor.1.refs_1_, f32[256,256]{1,0:T(8,128)S(1)} %get-tuple-element.47.refs_2_, f32[256,256]{1,0:T(8,128)S(1)} %collective-permute-done.11.refs_3_, f32[256,256]{1,0:T(8,128)S(1)} %collective-permute-done.12.refs_4_, ...), custom_call_target="tpu_custom_call" | custom-call | bytes 7200000 | tf_op jit(solution)/shard_map/finish/pallas_call | solution.py:230
  (4 shorter events, 0.0 us)
Async XLA Ops:
  2.3 20.0 %all-to-all-start = ((f32[16,80,128]{2,1,0:T(8,128)}), f32[16,80,128]{2,1,0:T(8,128)S(1)}, u32[]{:S(2)}, u32[]{:S(2)}) async-start(f32[16,80,128]{2,1,0:T(8,128)} %pieces.1), calls=%async_computation | async-start | bytes 1310720 | tf_op jit(solution)/shard_map/all_to_all | solution.py:274
  22.3 10.2 %collective-permute-start = (f32[2,80,128]{2,1,0:T(8,128)S(1)}, f32[2,80,128]{2,1,0:T(8,128)S(1)}, u32[]{:S(2)}, u32[]{:S(2)}) collective-permute-start(f32[2,80,128]{2,1,0:T(8,128)S(1)} %slice.4), channel_id=1, source_target_pairs={{0,16},{1,17},{2,18},{3,19},{4,20},{5,21},{6,22},{7,23},{8,24},{9,... | collective-permute-start | bytes 245768 | tf_op jit(solution)/shard_map/ppermute | solution.py:283
  33.8 22.6 %all-to-all-start.1 = ((f32[16,2,80,128]{3,2,1,0:T(8,128)}), f32[16,2,80,128]{3,2,1,0:T(8,128)S(1)}, u32[]{:S(2)}, u32[]{:S(2)}) async-start(f32[16,2,80,128]{3,2,1,0:T(8,128)} %broadcast_in_dim.11), calls=%async_computation.1 | async-start | bytes 2621440 | tf_op jit(solution)/shard_map/all_to_all | solution.py:274
  37.5 18.0 %collective-permute-start.1 = (f32[256,2,128]{2,1,0:T(2,128)}, f32[256,2,128]{2,1,0:T(2,128)S(1)}, u32[]{:S(2)}, u32[]{:S(2)}) collective-permute-start(f32[256,2,128]{2,1,0:T(2,128)} %refs_0_.1), channel_id=1, source_target_pairs={{64,0},{96,32},{65,1},{97,33},{66,2},{98,34},{67,3},{99,35},{68,4}... | collective-permute-start | bytes 786440 | tf_op jit(solution)/shard_map/ppermute | solution.py:317
  40.4 19.3 %collective-permute-start.3 = (f32[256,2,128]{2,1,0:T(2,128)}, f32[256,2,128]{2,1,0:T(2,128)}, u32[]{:S(2)}, u32[]{:S(2)}) collective-permute-start(f32[256,2,128]{2,1,0:T(2,128)} %refs_0_.1), channel_id=1, source_target_pairs={{128,0},{160,32},{129,1},{161,33},{130,2},{162,34},{131,3},{163,35... | collective-permute-start | bytes 786440 | tf_op jit(solution)/shard_map/ppermute | solution.py:317
  41.8 17.9 %collective-permute-start.4 = (f32[256,2,128]{2,1,0:T(2,128)}, f32[256,2,128]{2,1,0:T(2,128)}, u32[]{:S(2)}, u32[]{:S(2)}) collective-permute-start(f32[256,2,128]{2,1,0:T(2,128)} %refs_0_.1), channel_id=1, source_target_pairs={{192,0},{224,32},{193,1},{225,33},{194,2},{226,34},{195,3},{227,35... | collective-permute-start | bytes 786440 | tf_op jit(solution)/shard_map/ppermute | solution.py:317
  48.7 1.3 %copy-start = (bf16[4,256,1024]{2,1,0:T(8,128)(2,1)}, bf16[4,256,1024]{2,1,0:T(8,128)(2,1)S(1)}, u32[]{:S(2)}) copy-start(bf16[4,256,1024]{2,1,0:T(8,128)(2,1)S(1)} %get-tuple-element.44.alo_ref) | copy-start | bytes 6291460
  50.0 1.3 %copy-start.2 = (bf16[4,256,1024]{2,1,0:T(8,128)(2,1)}, bf16[4,256,1024]{2,1,0:T(8,128)(2,1)S(1)}, u32[]{:S(2)}) copy-start(bf16[4,256,1024]{2,1,0:T(8,128)(2,1)S(1)} %get-tuple-element.40.ahi_ref) | copy-start | bytes 6291460
  51.3 1.4 %copy-start.4 = (bf16[4,256,1024]{2,1,0:T(8,128)(2,1)}, bf16[4,256,1024]{2,1,0:T(8,128)(2,1)S(1)}, u32[]{:S(2)}) copy-start(bf16[4,256,1024]{2,1,0:T(8,128)(2,1)S(1)} %get-tuple-element.41.alo_ref) | copy-start | bytes 6291460
  55.5 0.7 copy-start.6
  56.4 3.3 %copy-start.3 = (bf16[4,256,1024]{2,1,0:T(8,128)(2,1)S(1)}, bf16[4,256,1024]{2,1,0:T(8,128)(2,1)}, u32[]{:S(2)}) copy-start(bf16[4,256,1024]{2,1,0:T(8,128)(2,1)} %copy-done.2) | copy-start | bytes 6291460
  58.3 1.4 %collective-permute-start.2 = (f32[192,128]{1,0:T(8,128)S(1)}, f32[192,128]{1,0:T(8,128)S(1)}, u32[]{:S(2)}, u32[]{:S(2)}) collective-permute-start(f32[192,128]{1,0:T(8,128)S(1)} %get-tuple-element.34), channel_id=1, source_target_pairs={{0,32},{32,0},{64,96},{96,64},{128,160},{160,128},{192,224},{224,1... | collective-permute-start | bytes 294920 | tf_op jit(solution)/shard_map/ppermute | solution.py:280
  59.7 1.6 %copy-start.5 = (bf16[4,256,1024]{2,1,0:T(8,128)(2,1)S(1)}, bf16[4,256,1024]{2,1,0:T(8,128)(2,1)}, u32[]{:S(2)}) copy-start(bf16[4,256,1024]{2,1,0:T(8,128)(2,1)} %copy-done.4) | copy-start | bytes 6291460
  61.3 9.5 %copy-start.1 = (bf16[4,256,1024]{2,1,0:T(8,128)(2,1)S(1)}, bf16[4,256,1024]{2,1,0:T(8,128)(2,1)}, u32[]{:S(2)}) copy-start(bf16[4,256,1024]{2,1,0:T(8,128)(2,1)} %copy-done) | copy-start | bytes 6291460
  63.7 12.0 %collective-permute-start.9 = (f32[4,256,256]{2,1,0:T(8,128)S(1)}, f32[4,256,256]{2,1,0:T(8,128)S(1)}, u32[]{:S(2)}, u32[]{:S(2)}) collective-permute-start(f32[4,256,256]{2,1,0:T(8,128)S(1)} %product_send.1), channel_id=1, source_target_pairs={{0,32},{32,0},{64,96},{96,64},{128,160},{160,128},{192,224},{224,1... | collective-permute-start | bytes 3145736 | tf_op jit(solution)/shard_map/ppermute | solution.py:280
  63.9 9.2 %collective-permute-start.10 = (f32[256,256]{1,0:T(8,128)S(1)}, f32[256,256]{1,0:T(8,128)S(1)}, u32[]{:S(2)}, u32[]{:S(2)}) collective-permute-start(f32[256,256]{1,0:T(8,128)S(1)} %get-tuple-element.45.own_ref), channel_id=1, source_target_pairs={{0,32},{1,33},{2,34},{3,35},{4,36},{5,37},{6,38},{7,39},{8,40},{9,... | collective-permute-start | bytes 786440 | tf_op jit(solution)/shard_map/ppermute | solution.py:346
  64.6 13.9 %collective-permute-start.7 = (f32[192,128]{1,0:T(8,128)S(1)}, f32[192,128]{1,0:T(8,128)S(1)}, u32[]{:S(2)}, u32[]{:S(2)}) collective-permute-start(f32[192,128]{1,0:T(8,128)S(1)} %add.17), channel_id=1, source_target_pairs={{0,192},{32,224},{64,128},{96,160},{128,64},{160,96},{192,0},{224,... | collective-permute-start | bytes 294920 | tf_op jit(solution)/shard_map/ppermute | solution.py:280
  65.7 14.3 %collective-permute-start.6 = (f32[192,128]{1,0:T(8,128)S(1)}, f32[192,128]{1,0:T(8,128)S(1)}, u32[]{:S(2)}, u32[]{:S(2)}) collective-permute-start(f32[192,128]{1,0:T(8,128)S(1)} %add.17), channel_id=1, source_target_pairs={{0,128},{32,160},{64,192},{96,224},{128,0},{160,32},{192,64},{224,... | collective-permute-start | bytes 294920 | tf_op jit(solution)/shard_map/ppermute | solution.py:280
  70.8 9.3 %collective-permute-start.5 = (f32[192,128]{1,0:T(8,128)S(1)}, f32[192,128]{1,0:T(8,128)S(1)}, u32[]{:S(2)}, u32[]{:S(2)}) collective-permute-start(f32[192,128]{1,0:T(8,128)S(1)} %add.17), channel_id=1, source_target_pairs={{0,64},{32,96},{64,0},{96,32},{128,192},{160,224},{192,128},{224,1... | collective-permute-start | bytes 294920 | tf_op jit(solution)/shard_map/ppermute | solution.py:280
  70.8 2.4 %copy-start.7 = (f32[256,2,128]{2,1,0:T(2,128)S(1)}, f32[256,2,128]{2,1,0:T(2,128)}, u32[]{:S(2)}) copy-start(f32[256,2,128]{2,1,0:T(2,128)} %copy-done.6) | copy-start | bytes 786436
  76.4 18.3 %collective-permute-start.11 = (f32[256,256]{1,0:T(8,128)S(1)}, f32[256,256]{1,0:T(8,128)S(1)}, u32[]{:S(2)}, u32[]{:S(2)}) collective-permute-start(f32[256,256]{1,0:T(8,128)S(1)} %get-tuple-element.48), channel_id=1, source_target_pairs={{0,64},{32,96},{64,0},{96,32},{128,192},{160,224},{192,128},{224,1... | collective-permute-start | bytes 786440 | tf_op jit(solution)/shard_map/ppermute | solution.py:280
  78.5 18.0 %collective-permute-start.12 = (f32[256,256]{1,0:T(8,128)S(1)}, f32[256,256]{1,0:T(8,128)S(1)}, u32[]{:S(2)}, u32[]{:S(2)}) collective-permute-start(f32[256,256]{1,0:T(8,128)S(1)} %get-tuple-element.49), channel_id=1, source_target_pairs={{0,128},{32,160},{64,192},{96,224},{128,0},{160,32},{192,64},{224,... | collective-permute-start | bytes 786440 | tf_op jit(solution)/shard_map/ppermute | solution.py:280
  78.5 23.2 %collective-permute-start.13 = (f32[256,256]{1,0:T(8,128)S(1)}, f32[256,256]{1,0:T(8,128)S(1)}, u32[]{:S(2)}, u32[]{:S(2)}) collective-permute-start(f32[256,256]{1,0:T(8,128)S(1)} %get-tuple-element.50), channel_id=1, source_target_pairs={{0,192},{32,224},{64,128},{96,160},{128,64},{160,96},{192,0},{224,... | collective-permute-start | bytes 786440 | tf_op jit(solution)/shard_map/ppermute | solution.py:280
  80.1 1.4 %collective-permute-start.8 = (f32[192,128]{1,0:T(8,128)S(1)}, f32[192,128]{1,0:T(8,128)S(1)}, u32[]{:S(2)}, u32[]{:S(2)}) collective-permute-start(f32[192,128]{1,0:T(8,128)S(1)} %add_add_fusion.kept_ref), channel_id=1, source_target_pairs={{0,32},{32,0},{64,96},{96,64},{128,160},{160,128},{192,224},{224,1... | collective-permute-start | bytes 294920 | tf_op jit(solution)/shard_map/ppermute | solution.py:280
